TPU v7x, 128 devices: a whole 4x4x4 slice. The times are simulated.
128 devices in a mesh: sub: 32 (over y, x, core), blk: 4 (over z).
Axes of the slice: x: 4, y: 4, z: 4, core: 2. Of those that a mesh axis runs over, the one named last changes fastest.
Arguments:
- coupling_blocks: float32 [256, 16, 9, 128, 128], P(('sub', 'blk')), may hold values from -0.12053519 to 1.3637
- block_inverse: float32 [256, 16, 128, 128], P(('sub', 'blk')), may hold values from -0.044194174 to 1.5, as said below
- coupling_pattern: int32 [256, 16, 9], P(('sub', 'blk')), may hold values 0 or 1
- link_blocks: int32 [256, 8], P(('sub', 'blk')), may hold values from 4 to 63, as said below
- interface_panel: float32 [8192, 512], P('sub', 'blk'), may hold values from -0.5 to 1.04, as said below
Outputs:
- panel_factor: float32 [8192, 512], P('sub', 'blk')
Inputs may be any that keep to these rules, and one draw needn't show every extreme that they name: `block_inverse`: every block is symmetric. `link_blocks`: each row names 8 different interface blocks, none of the panel's first 4. `interface_panel`: the first 512 rows are symmetric.
All inputs are finite; a program needn't handle non-finite values. No bound on the sum of `coupling_pattern` on one device may be relied on, other than what follows from the above.
Results may differ from a plain program's by a relative error of at most 0.000075.
Values sent between devices are 32-bit elements; how exact they have to be, the bound alone decides.
A program may use at most 128 MiB of HBM per device.

v0:
```python
import jax
import jax.numpy as jnp
from jax import lax
from jax.sharding import PartitionSpec as P

HIGHEST = lax.Precision.HIGHEST


def passed_along(block, axis, distance):
    devices = range(lax.axis_size(axis))
    route = [(i - distance, i) for i in devices if i - distance in devices]
    return lax.ppermute(block, axis, route)


def shards(coupling_blocks, block_inverse, coupling_pattern, link_blocks, interface_panel):
    sub_count = lax.axis_size("sub")
    sub_place = lax.axis_index("sub")
    blk_count = lax.axis_size("blk")
    blk_place = lax.axis_index("blk")
    row_count = interface_panel.shape[0]
    block_width = interface_panel.shape[1]
    total_rows = row_count * sub_count
    block_total = total_rows // block_width
    panel_width = block_width * blk_count
    local_count = coupling_blocks.shape[0]
    masked = coupling_blocks * coupling_pattern.astype(jnp.float32)[:, :, :, None, None]
    solved = jnp.einsum("ncjk,ncik->ncji", block_inverse, masked[:, :, 0], precision=HIGHEST)
    updates = jnp.einsum("nclij,ncjk->nlik", masked, solved, precision=HIGHEST)
    updates = updates.reshape(-1, block_width, block_width)
    own_block = jnp.full((local_count, 1), blk_place, jnp.int32)
    row_blocks = jnp.concatenate([own_block, link_blocks], axis=1).reshape(-1)
    selector = (jnp.arange(block_total, dtype=jnp.int32)[:, None] == row_blocks[None, :]).astype(
        jnp.float32
    )
    placed_rows = jnp.einsum("gk,kic->gic", selector, updates, precision=HIGHEST)
    own_rows = interface_panel - lax.psum_scatter(
        placed_rows.reshape(row_count * lax.axis_size("sub"), block_width),
        "sub",
        scatter_dimension=0,
        tiled=True,
    )
    padded = jnp.zeros((panel_width + row_count, block_width), jnp.float32)
    offset = jnp.minimum(sub_place * row_count, panel_width)
    diag_column = lax.psum(
        lax.dynamic_update_slice_in_dim(padded, own_rows, offset, 0)[:panel_width], "sub"
    )
    diag_block = lax.all_gather(diag_column, "blk", axis=1, tiled=True)
    diag_factor = jnp.linalg.cholesky(diag_block)
    block_rows = lax.dynamic_slice_in_dim(diag_factor, blk_place * block_width, block_width, 0)
    pivot_block = lax.dynamic_slice_in_dim(block_rows, blk_place * block_width, block_width, 1)

    def finish(earlier):
        reduced = own_rows - jnp.dot(
            earlier, block_rows.T, precision=HIGHEST, preferred_element_type=jnp.float32
        )
        return lax.linalg.triangular_solve(
            pivot_block, reduced, left_side=False, lower=True, transpose_a=True
        )

    earlier = jnp.zeros((row_count, panel_width), jnp.float32)
    for turn_index in range(blk_count - 1):
        filled = lax.dynamic_update_slice_in_dim(
            earlier, finish(earlier), blk_place * block_width, 1
        )
        earlier = passed_along(filled, "blk", 1)
    result = finish(earlier)
    return result


def solution(mesh):
    in_specs = (
        P(("sub", "blk"), None, None, None, None),
        P(("sub", "blk"), None, None, None),
        P(("sub", "blk"), None, None),
        P(("sub", "blk"), None),
        P("sub", "blk"),
    )
    out_specs = P("sub", "blk")
    return jax.shard_map(shards, mesh=mesh, in_specs=in_specs, out_specs=out_specs, check_vma=False)
```

profile of v0, /device:TPU:64, one launch (start us, length us, event | category | flops | bytes accessed | tf_op | source)
XLA Modules:
  0.0 417.3 jit_solution(10821319696839535440)
XLA Ops:
  7.5 7.1 %broadcast_multiply_fusion = f32[2,16,9,128,128]{4,3,2,1,0:T(8,128)S(1)} fusion(f32[2,16,9,128,128]{4,3,2,1,0:T(8,128)} %param.7, f32[2,16,9]{2,1,0:T(8,128)S(1)} %copy.6), kind=kLoop, calls=%fused_computation | loop fusion | flops 4718592 | bytes 37749888 | tf_op jit(solution)/shard_map/mul | solution.py:26
  14.6 4.5 %fusion = f32[2,16,128,128]{2,3,1,0:T(8,128)S(1)} fusion(f32[2,16,128,128]{3,2,1,0:T(8,128)S(1)} %copy-done, f32[2,16,9,128,128]{4,3,2,1,0:T(8,128)S(1)} %broadcast_multiply_fusion), kind=kOutput, calls=%fused_computation.3 | convolution fusion | flops 805306368 | bytes 6291456 | tf_op jit(solution)/shard_map/ncjk,ncik->ncji/dot_general | solution.py:27
  19.1 16.6 %fusion.1 = f32[2,9,128,128,1]{3,2,1,4,0:T(8,128)S(1)} fusion(f32[2,16,9,128,128]{4,3,2,1,0:T(8,128)S(1)} %broadcast_multiply_fusion, f32[2,16,128,128]{2,3,1,0:T(8,128)S(1)} %fusion), kind=kOutput, calls=%fused_computation.4 | convolution fusion | flops 7247757312 | bytes 22151168 | tf_op jit(solution)/shard_map/nclij,ncjk->nlik/dot_general | solution.py:28
  35.7 1.6 copy.18
  37.5 3.3 fusion.34
  40.8 5.2 %copy.25 = f32[16,8,64,128]{3,1,2,0:T(8,128)} copy(f32[16,8,64,128]{3,2,1,0:T(8,128)S(1)} %bitcast.88) | data formatting | bytes 8388608
  47.0 82.6 %reduce-scatter.2.cloned.1.call-done = f32[256,128]{0,1:T(8,128)} async-done(((f32[8192,128]{0,1:T(8,128)}), f32[256,128]{0,1:T(8,128)}) %reduce-scatter.2.cloned.1.call-update) | async-done | bytes 131088 | tf_op jit(solution)/shard_map/reduce_scatter | solution.py:36
  130.6 1.1 dynamic_update_slice.12
  132.9 100.9 %all-reduce.4.cloned.1.call-done = f32[512,128]{0,1:T(8,128)} async-done(((f32[512,128]{0,1:T(8,128)}), f32[512,128]{0,1:T(8,128)}) %all-reduce.4.cloned.1.call-update) | async-done | bytes 262160 | tf_op jit(solution)/shard_map/psum | solution.py:44
  233.8 24.7 %all-gather.2.cloned.1.call-done = f32[512,512]{0,1:T(8,128)} async-done(((f32[512,128]{0,1:T(8,128)}), f32[512,512]{0,1:T(8,128)}) %all-gather.2.cloned.1.call-update) | async-done | bytes 1048592 | tf_op jit(solution)/shard_map/all_gather | solution.py:47
  258.5 2.7 copy.11
  261.2 1.4 fusion.6
  263.6 11.7 %cholesky.104 = f32[128,128]{1,0:T(8,128)S(1)} custom-call(f32[128,128]{1,0:T(8,128)S(1)} %cholesky.266), custom_call_target="Cholesky" | custom-call | tf_op jit(solution)/shard_map/jit(cholesky)/cholesky | solution.py:48
  275.5 9.8 %custom-call.30 = f32[1,128,128]{1,2,0:T(8,128)S(1)} custom-call(f32[1,128,128]{2,1,0:T(8,128)S(1)} %get-tuple-element.15), custom_call_target="InvertDiagBlocksLowerTriangular" | custom-call | tf_op jit(solution)/shard_map/jit(cholesky)/cholesky | solution.py:48
  285.3 1.3 fusion.12
  287.5 1.4 convolution_subtract_fusion
  289.6 11.7 %cholesky.217 = f32[128,128]{1,0:T(8,128)S(1)} custom-call(f32[128,128]{1,0:T(8,128)S(1)} %cholesky.270), custom_call_target="Cholesky" | custom-call | tf_op jit(solution)/shard_map/jit(cholesky)/cholesky | solution.py:48
  302.3 10.0 %custom-call.31 = f32[1,128,128]{1,2,0:T(8,128)S(1)} custom-call(f32[1,128,128]{2,1,0:T(8,128)S(1)} %get-tuple-element.12), custom_call_target="InvertDiagBlocksLowerTriangular" | custom-call | tf_op jit(solution)/shard_map/jit(cholesky)/cholesky | solution.py:48
  312.2 1.2 convolution_dynamic-update-slice_fusion
  313.4 1.3 convolution_subtract_fusion.4
  314.7 11.7 %cholesky.238 = f32[128,128]{1,0:T(8,128)S(1)} custom-call(f32[128,128]{1,0:T(8,128)S(1)} %cholesky.275), custom_call_target="Cholesky" | custom-call | tf_op jit(solution)/shard_map/jit(cholesky)/cholesky | solution.py:48
  327.2 9.8 %custom-call.32 = f32[1,128,128]{1,2,0:T(8,128)S(1)} custom-call(f32[1,128,128]{2,1,0:T(8,128)S(1)} %get-tuple-element.9), custom_call_target="InvertDiagBlocksLowerTriangular" | custom-call | tf_op jit(solution)/shard_map/jit(cholesky)/cholesky | solution.py:48
  337.2 1.2 convolution_subtract_fusion.5
  338.4 11.9 %cholesky.255 = f32[128,128]{1,0:T(8,128)S(1)} custom-call(f32[128,128]{1,0:T(8,128)S(1)} %convolution_subtract_fusion.5), custom_call_target="Cholesky" | custom-call | tf_op jit(solution)/shard_map/jit(cholesky)/cholesky | solution.py:48
  355.5 9.8 %custom-call.39 = f32[1,128,128]{1,2,0:T(8,128)S(1)} custom-call(f32[1,128,128]{2,1,0:T(8,128)S(1)} %select_bitcast_fusion), custom_call_target="InvertDiagBlocksLowerTriangular" | custom-call | tf_op jit(solution)/shard_map/triangular_solve/custom-call.3 | solution.py:56
  365.8 2.7 collective-permute-start
  368.5 11.8 %collective-permute-done = f32[256,512]{0,1:T(8,128)S(1)} collective-permute-done((f32[256,512]{0,1:T(8,128)S(1)}, f32[256,512]{0,1:T(8,128)S(1)}, u32[]{:S(2)}, u32[]{:S(2)}) %collective-permute-start) | collective-permute-done | bytes 524320 | tf_op jit(solution)/shard_map/ppermute | solution.py:12
  380.3 1.4 convolution_subtract_fusion.3
  382.0 2.7 collective-permute-start.1
  384.7 10.9 %collective-permute-done.1 = f32[256,512]{0,1:T(8,128)S(1)} collective-permute-done((f32[256,512]{0,1:T(8,128)S(1)}, f32[256,512]{0,1:T(8,128)S(1)}, u32[]{:S(2)}, u32[]{:S(2)}) %collective-permute-start.1) | collective-permute-done | bytes 524320 | tf_op jit(solution)/shard_map/ppermute | solution.py:12
  396.3 2.6 collective-permute-start.2
  399.0 10.0 %collective-permute-done.2 = f32[256,512]{0,1:T(8,128)S(1)} collective-permute-done((f32[256,512]{0,1:T(8,128)S(1)}, f32[256,512]{0,1:T(8,128)S(1)}, u32[]{:S(2)}, u32[]{:S(2)}) %collective-permute-start.2) | collective-permute-done | bytes 524320 | tf_op jit(solution)/shard_map/ppermute | solution.py:12
  (55 shorter events, 14.4 us)
Async XLA Ops:
  6.5 8.1 %copy-start = (f32[2,16,128,128]{3,2,1,0:T(8,128)S(1)}, f32[2,16,128,128]{3,2,1,0:T(8,128)}, u32[]{:S(2)}) copy-start(f32[2,16,128,128]{3,2,1,0:T(8,128)} %param.8) | copy-start | bytes 6291460
  6.5 123.1 %reduce-scatter.2.cloned.1.call-start = ((), (), s32[]{:S(2)}) async-start(), calls=%async_computation.1 | async-start | bytes 4325376 | tf_op jit(solution)/shard_map/reduce_scatter | solution.py:36
  35.7 1.6 copy-start.7
  46.0 0.9 copy-start.6
  46.0 187.7 %all-reduce.4.cloned.1.call-start = ((), (), s32[]{:S(2)}) async-start(), calls=%async_computation.2 | async-start | bytes 524288 | tf_op jit(solution)/shard_map/psum | solution.py:44
  132.5 126.0 %all-gather.2.cloned.1.call-start = ((), (), s32[]{:S(2)}) async-start(), calls=%async_computation.3 | async-start | bytes 1310720 | tf_op jit(solution)/shard_map/all_gather | solution.py:47
  258.5 2.7 copy-start.3
  262.6 1.0 copy-start.4
  288.9 0.7 copy-start.5
  354.4 1.0 copy-start.1
  355.5 40.0 %copy-start.2 = (f32[512,512]{1,0:T(8,128)S(1)}, f32[512,512]{1,0:T(8,128)}, u32[]{:S(2)}) copy-start(f32[512,512]{1,0:T(8,128)} %copy-done.1) | copy-start | bytes 3145732
  365.8 14.5 %collective-permute-start = (f32[256,512]{0,1:T(8,128)S(1)}, f32[256,512]{0,1:T(8,128)S(1)}, u32[]{:S(2)}, u32[]{:S(2)}) collective-permute-start(f32[256,512]{0,1:T(8,128)S(1)} %fusion.5), channel_id=1, source_target_pairs={{0,1},{1,2},{2,3},{4,5},{5,6},{6,7},{8,9},{9,10},{10,11},{12,13},{... | collective-permute-start | bytes 1572872 | tf_op jit(solution)/shard_map/ppermute | solution.py:12
  382.0 13.6 %collective-permute-start.1 = (f32[256,512]{0,1:T(8,128)S(1)}, f32[256,512]{0,1:T(8,128)S(1)}, u32[]{:S(2)}, u32[]{:S(2)}) collective-permute-start(f32[256,512]{0,1:T(8,128)S(1)} %fusion.4), channel_id=1, source_target_pairs={{0,1},{1,2},{2,3},{4,5},{5,6},{6,7},{8,9},{9,10},{10,11},{12,13},{... | collective-permute-start | bytes 1572872 | tf_op jit(solution)/shard_map/ppermute | solution.py:12
  396.3 12.7 %collective-permute-start.2 = (f32[256,512]{0,1:T(8,128)S(1)}, f32[256,512]{0,1:T(8,128)S(1)}, u32[]{:S(2)}, u32[]{:S(2)}) collective-permute-start(f32[256,512]{0,1:T(8,128)S(1)} %fusion.3), channel_id=1, source_target_pairs={{0,1},{1,2},{2,3},{4,5},{5,6},{6,7},{8,9},{9,10},{10,11},{12,13},{... | collective-permute-start | bytes 1572872 | tf_op jit(solution)/shard_map/ppermute | solution.py:12
Sparse Core Ops, SparseCore 0:
  46.2 83.4 reduce-scatter.1
  133.2 100.5 all-reduce.3
  235.5 22.9 all-gather.1
where the time goes:
time: 424 us; the launch traced here: 417 us
  waiting for transfers between devices  241 us (57%)
  other arithmetic  99.3 us (23%)
  matrix products  34.5 us (8%)
  local copies, waits for them, and re-layouts  17.7 us (4%)
  between operations  16.3 us (4%)
  starting transfers between devices  8.53 us (2%)
    psum x1, waiting for transfers between devices, shards(): lax.psum(lax.dynamic_update_slice_in_dim(padded, own_rows, offset, 0)[:pa...  101 us
    reduce_scatter x1, waiting for transfers between devices, shards(): lax.psum_scatter(placed_rows.reshape(row_count * lax.axis_size('sub'), bl...  82.6 us
    another operation x14, other arithmetic, shards(): diag_factor = jnp.linalg.cholesky(diag_block)  78.8 us
    ppermute x3, waiting for transfers between devices, passed_along(): return lax.ppermute(block, axis, route)  32.7 us
    all_gather x1, waiting for transfers between devices, shards(): diag_block = lax.all_gather(diag_column, 'blk', axis=1, tiled=True)  24.7 us
    dot_general x1, matrix products, shards(): updates = jnp.einsum('nclij,ncjk->nlik', masked, solved, precision=HIGHEST)  16.6 us
    another operation x2, other arithmetic, finish(): lax.linalg.triangular_solve(pivot_block, reduced, left_side=False, lower=...  9.9 us
    unnamed x18, local copies, waits for them, and re-layouts  8.65 us
  transfers between devices with their start and end apart: 6, of which 6 were waited for; matrix products, arithmetic and copies ran while one was open for 0% of the time, Pallas kernels for 0%

commit v1 on v0

v1 whole, which is shorter than its diff:
```python
import functools

import jax
import jax.numpy as jnp
from jax import lax
from jax.experimental import pallas as pl
from jax.experimental.pallas import tpu as pltpu
from jax.sharding import PartitionSpec as P

F32 = jnp.float32
BF16 = jnp.bfloat16
MESH = pl.DeviceIdType.MESH
BLK = 128
CHUNK = 4
STEP = 16
OFF = ((1, 0), (2, 0), (3, 0), (2, 1), (3, 1), (3, 2))
OFF_AT = {pair: k for k, pair in enumerate(OFF)}


def halves(value):
    high = value.astype(BF16)
    return high, (value - high.astype(F32)).astype(BF16)


def product_nt(a, b):
    ah, al = halves(a)
    bh, bl = halves(b)
    return lax.dot_general(
        jnp.concatenate([ah, al, ah], axis=1),
        jnp.concatenate([bh, bh, bl], axis=1),
        (((1,), (1,)), ((), ())),
        preferred_element_type=F32,
    )


def product_nn(a, b):
    ah, al = halves(a)
    bh, bl = halves(b)
    return jnp.dot(
        jnp.concatenate([ah, al, ah], axis=1),
        jnp.concatenate([bh, bh, bl], axis=0),
        preferred_element_type=F32,
    )


def update_kernel(
    pattern_ref, link_ref, coupling_ref, inverse_ref,
    first_ref, links_ref, slot_ref,
    cbuf, ibuf, lhs, rhs, acc, csem, isem,
):
    subs, cells = coupling_ref.shape[0], coupling_ref.shape[1]
    faces = coupling_ref.shape[2]
    links = faces - 1
    none = subs * links
    rows = faces * BLK

    def fetch(i, carry):
        n, c = i // cells, lax.rem(i, cells)
        pltpu.make_async_copy(inverse_ref.at[n, c], ibuf.at[i], isem.at[i]).start()
        pltpu.make_async_copy(coupling_ref.at[n, c], cbuf.at[i], csem.at[i]).start()
        return carry

    lax.fori_loop(0, subs * cells, fetch, 0)

    def clear(i, carry):
        for n in range(subs):
            slot_ref[n, i] = none
        return carry

    lax.fori_loop(0, slot_ref.shape[1], clear, 0)
    for n in range(subs):
        for l in range(links):
            slot_ref[n, link_ref[n, l]] = n * links + l
    links_ref[none] = jnp.zeros((BLK, BLK), F32)

    for n in range(subs):
        def chunk_step(chunk, carry):
            for k in range(CHUNK):
                cell = chunk * CHUNK + k
                i = n * cells + cell
                pltpu.make_async_copy(inverse_ref.at[n, cell], ibuf.at[i], isem.at[i]).wait()
                pltpu.make_async_copy(coupling_ref.at[n, cell], cbuf.at[i], csem.at[i]).wait()
                for l in range(faces):
                    block = cbuf[i, l] * pattern_ref[n, cell, l].astype(F32)
                    high, low = halves(block)
                    if l == 0:
                        solved = product_nt(ibuf[i], block)
                    place = pl.ds(l * BLK, BLK)
                    lhs[place, pl.ds(k * 2 * BLK, BLK)] = high
                    lhs[place, pl.ds(k * 2 * BLK + BLK, BLK)] = low
                sh, sl = halves(solved)
                rhs[pl.ds(k * 2 * BLK, BLK), :] = jnp.concatenate([sh, sl], axis=1)
                rhs[pl.ds(k * 2 * BLK + BLK, BLK), :] = jnp.concatenate([sh, jnp.zeros_like(sl)], axis=1)
            part = jnp.dot(lhs[...], rhs[...], preferred_element_type=F32)

            @pl.when(chunk == 0)
            def _():
                acc[...] = part

            @pl.when(chunk > 0)
            def _():
                acc[...] += part

            return carry

        lax.fori_loop(0, cells // CHUNK, chunk_step, 0)
        total = acc[:, :BLK] + acc[:, BLK:]
        if n == 0:
            first_ref[...] = total[:BLK]
        else:
            first_ref[...] += total[:BLK]
        links_ref[n * links : (n + 1) * links] = total[BLK:].reshape(links, BLK, BLK)


def local_updates(coupling_blocks, block_inverse, coupling_pattern, link_blocks, block_rows):
    subs, cells, faces = coupling_blocks.shape[:3]
    rows = faces * BLK
    return pl.pallas_call(
        update_kernel,
        out_shape=(
            jax.ShapeDtypeStruct((BLK, BLK), F32),
            jax.ShapeDtypeStruct((subs * (faces - 1) + 1, BLK, BLK), F32),
            jax.ShapeDtypeStruct((subs, block_rows), jnp.int32),
        ),
        in_specs=[
            pl.BlockSpec(memory_space=pltpu.SMEM),
            pl.BlockSpec(memory_space=pltpu.SMEM),
            pl.BlockSpec(memory_space=pl.ANY),
            pl.BlockSpec(memory_space=pl.ANY),
        ],
        out_specs=(
            pl.BlockSpec(memory_space=pltpu.VMEM),
            pl.BlockSpec(memory_space=pltpu.VMEM),
            pl.BlockSpec(memory_space=pltpu.SMEM),
        ),
        scratch_shapes=[
            pltpu.VMEM((subs * cells, faces, BLK, BLK), F32),
            pltpu.VMEM((subs * cells, BLK, BLK), F32),
            pltpu.VMEM((rows, CHUNK * 2 * BLK), BF16),
            pltpu.VMEM((CHUNK * 2 * BLK, 2 * BLK), BF16),
            pltpu.VMEM((rows, 2 * BLK), F32),
            pltpu.SemaphoreType.DMA((subs * cells,)),
            pltpu.SemaphoreType.DMA((subs * cells,)),
        ],
        compiler_params=pltpu.CompilerParams(vmem_limit_bytes=48 << 20),
        name="local_updates",
    )(coupling_pattern, link_blocks, coupling_blocks, block_inverse)


def inverse_factor(pair):
    rows = lax.broadcasted_iota(jnp.int32, (STEP, BLK), 0)
    for r in range(0, BLK, STEP):
        pa, pe = pair[r : r + STEP, :BLK], pair[r : r + STEP, BLK:]
        t = jnp.stack([jnp.broadcast_to(pa[:, r + j : r + j + 1], (STEP, BLK)) for j in range(STEP)])
        for k in range(STEP):
            scale = lax.rsqrt(t[0, k : k + 1, :])
            m = jnp.where(rows > k, t[0] * scale, 0.0)
            if k + 1 < STEP:
                t = t[1:] - m[None] * (t[1:, k : k + 1, :] * scale[None])
            ra, re = pa[k : k + 1] * scale, pe[k : k + 1] * scale
            pa = jnp.where(rows == k, ra, pa - m * ra)
            pe = jnp.where(rows == k, re, pe - m * re)
        pair[r : r + STEP, BLK:] = pe
        if r + STEP < BLK:
            high, low = halves(jnp.concatenate([pa, pe], axis=1))
            ah, al = high[:, :BLK], low[:, :BLK]
            change = lax.dot_general(
                jnp.concatenate([ah, ah, al], axis=0),
                jnp.concatenate([high, low, high], axis=0),
                (((0,), (0,)), ((), ())),
                preferred_element_type=F32,
            )
            pair[r + STEP :, :] = pair[r + STEP :, :] - change[r + STEP :, :]


def panel_kernel(
    nx, slot_ref, first_ref, links_ref, panel_ref, out_ref,
    firstc, gather1, gather2, piece, diag, offpiece, off,
    send0, recv0, acc, relay_r, relay_l, direct_r, direct_l, onward_r, onward_l,
    last, sall, pair, lower, inv, vz, top,
    d1s, d1r, d2s, d2r, d3s, d3r, sc_s, op_r, fw_s, oa_s, oa_r,
    s0s, s0r, s1s, s1r, s2s, s2r, zs, zr,
):
    sub, z = lax.axis_index("sub"), lax.axis_index("blk")
    core = lax.rem(sub, 2)
    x = lax.rem(sub // 2, nx)
    y = sub // (2 * nx)

    def sub_of(yy, xx, cc):
        return (yy * nx + xx) * 2 + cc

    def remote(src, dst, ssem, rsem, to_sub, to_z):
        return pltpu.make_async_remote_copy(
            src_ref=src, dst_ref=dst, send_sem=ssem, recv_sem=rsem,
            device_id=(to_sub, to_z), device_id_type=MESH,
        )

    place = (core * 4 + x) * 4 + z

    def plane_peer(t):
        e = lax.rem(place + t, 32)
        q = e // 4
        return sub_of(y, lax.rem(q, 4), q // 4), lax.rem(e, 4)

    barrier = pltpu.get_barrier_semaphore()

    def greet(t, carry):
        to_sub, to_z = plane_peer(t)
        pl.semaphore_signal(barrier, inc=1, device_id=(to_sub, to_z), device_id_type=MESH)
        return carry

    lax.fori_loop(1, 32, greet, 0)

    def greet_y(t, carry):
        pl.semaphore_signal(
            barrier, inc=1, device_id=(sub_of(lax.rem(y + t, 4), x, core), z), device_id_type=MESH
        )
        return carry

    lax.fori_loop(1, 4, greet_y, 0)

    firstc[...] = -first_ref[...]

    @pl.when(sub == z // 2)
    def _():
        firstc[...] += panel_ref[pl.ds(pl.multiple_of(lax.rem(z, 2) * BLK, BLK), BLK), :]

    pl.semaphore_wait(barrier, 34)

    q = core * 4 + x

    def d1_copy(t):
        to = lax.rem(q + t, 8)
        return remote(
            firstc.at[pl.ds(pl.multiple_of(to * 16, 16), 16)], gather1.at[q],
            d1s.at[t], d1r.at[t], sub_of(y, lax.rem(to, 4), to // 4), z,
        )

    def d2_copy(t):
        return remote(
            gather2.at[y], gather2.at[y], d2s.at[t], d2r.at[t],
            sub_of(lax.rem(y + t, 4), x, core), z,
        )

    mine = pl.ds(pl.multiple_of(q * 16, 16), 16)

    def d3_copy(t):
        to_sub, to_z = plane_peer(t)
        return remote(piece, diag.at[z, mine], d3s.at[t], d3r, to_sub, to_z)

    def loop(low, high, make, *actions):
        def body(t, carry):
            copy = make(t)
            for action in actions:
                getattr(copy, action)()
            return carry

        lax.fori_loop(low, high, body, 0)

    loop(1, 8, d1_copy, "start")
    gather1[q] = firstc[mine, :]

    def scatter(action):
        for k, (i, j) in enumerate(OFF):
            @pl.when((sub == i // 2) & (z == j))
            def _(k=k, i=i, j=j):
                for xx in range(4):
                    src = panel_ref.at[pl.ds((i % 2) * BLK + xx * 32, 32)]
                    if xx == 0 and k % 2 == i // 2 and k // 2 == j:
                        if action == "start":
                            pltpu.make_async_copy(src, offpiece, op_r).start()
                    else:
                        copy = remote(
                            src, offpiece, sc_s.at[k * 4 + xx], op_r,
                            jnp.int32(xx * 2 + k % 2), jnp.int32(k // 2),
                        )
                        getattr(copy, action)()

    scatter("start")

    def placed(r, h, other, to_core):
        to_x = lax.rem(x + r, 4) if h == 0 else other
        to_y = other if h == 0 else lax.rem(y + r, 4)
        g = sub_of(to_y, to_x, to_core) * 2 + h
        return links_ref[slot_ref[0, g]] + links_ref[slot_ref[1, g]]

    def fill(ref, r, to_core):
        def body(other, carry):
            for h in range(2):
                ref[r, h, other] = placed(r, h, other, to_core)
            return carry

        lax.fori_loop(0, 4, body, 0)

    def s0_copy(r):
        return remote(send0.at[r], recv0.at[r], s0s.at[r], s0r.at[r], sub_of(y, x, 1 - core), z)

    for r in (2, 1):
        fill(send0, r, 1 - core)
        s0_copy(r).start()

    loop(1, 8, d1_copy, "wait_recv")
    gather2[y] = jnp.sum(gather1[...], axis=0)
    loop(1, 4, d2_copy, "start")

    for r in (3, 0):
        fill(send0, r, 1 - core)
        s0_copy(r).start()

    holder = z * 2 + core

    def fw_copy(t):
        return remote(offpiece, offpiece, fw_s.at[t], op_r, sub_of(lax.rem(y + t, 4), x, core), z)

    @pl.when(holder < 6)
    def _():
        pltpu.make_async_copy(offpiece, offpiece, op_r).wait()

    @pl.when((holder < 6) & (y == 0))
    def _():
        loop(1, 4, fw_copy, "start")

    loop(1, 4, d2_copy, "wait_recv")
    piece[...] = jnp.sum(gather2[...], axis=0)
    own_diag = pltpu.make_async_copy(piece, diag.at[z, mine], d3r)
    own_diag.start()
    loop(1, 32, d3_copy, "start")

    quarter = pl.ds(pl.multiple_of(x * 32, 32), 32)

    def oa_copy(t):
        to_sub, to_z = plane_peer(t)
        return remote(offpiece, off.at[holder, quarter], oa_s.at[t], oa_r, to_sub, to_z)

    @pl.when(holder < 6)
    def _():
        pltpu.make_async_copy(offpiece, off.at[holder, quarter], oa_r).start()
        loop(1, 32, oa_copy, "start")

    def ring(h, step):
        if h == 0:
            return sub_of(y, lax.rem(x + step + 4, 4), core)
        return sub_of(lax.rem(y + step + 4, 4), x, core)

    def s1_copy(kind, h):
        n = kind * 2 + h
        src, dst, step = (
            (acc.at[2, h, 0:2], relay_r.at[h], 1),
            (acc.at[2, h, 2:4], relay_l.at[h], -1),
            (acc.at[1, h, 2:4], direct_r.at[h], 1),
            (acc.at[3, h, 0:2], direct_l.at[h], -1),
            (acc.at[1, h, 0:2], onward_r.at[h], 1),
            (acc.at[3, h, 2:4], onward_l.at[h], -1),
        )[kind]
        return remote(src, dst, s1s.at[n], s1r.at[n], ring(h, step), z)

    def arrive0(r):
        fill(acc, r, core)
        s0_copy(r).wait_recv()
        acc[r] += recv0[r]

    def service0():
        arrive0(2)
        for h in range(2):
            s1_copy(0, h).start()
            s1_copy(1, h).start()
        arrive0(1)
        for h in range(2):
            s1_copy(2, h).start()
        arrive0(3)
        for h in range(2):
            s1_copy(3, h).start()
        arrive0(0)

    def service1():
        for h in range(2):
            s1_copy(0, h).wait_recv()
            acc[1, h, 0:2] += relay_r[h]
            s1_copy(4, h).start()
            s1_copy(1, h).wait_recv()
            acc[3, h, 2:4] += relay_l[h]
            s1_copy(5, h).start()

    def s2_copy(h, d):
        there = lax.rem((y if h == 0 else x) + d, 4)
        to = sub_of(there, x, core) if h == 0 else sub_of(y, there, core)
        n = h * 3 + d - 1
        return remote(acc.at[0, h, there], last.at[n], s2s.at[n], s2r.at[n], to, z)

    def service2():
        for h in range(2):
            s1_copy(4, h).wait_recv()
            s1_copy(3, h).wait_recv()
            acc[0, h, 0:2] += onward_r[h] + direct_l[h]
            s1_copy(2, h).wait_recv()
            s1_copy(5, h).wait_recv()
            acc[0, h, 2:4] += direct_r[h] + onward_l[h]
            for d in range(1, 4):
                s2_copy(h, d).start()

    def z_copy(d):
        return remote(sall.at[z], sall.at[z], zs.at[d], zr.at[d], sub, z + d)

    def service3():
        for h in range(2):
            total = acc[0, h, y if h == 0 else x]
            for d in range(1, 4):
                s2_copy(h, d).wait_recv()
                total = total + last[h * 3 + d - 1]
            rows = panel_ref[h * BLK : (h + 1) * BLK, :] - total
            sall[z, h * BLK : (h + 1) * BLK] = rows

            @pl.when(sub * 2 + h == z)
            def _():
                sall[z, h * BLK : (h + 1) * BLK] = top[...]

        for d in range(1, 4):
            @pl.when(z + d < 4)
            def _():
                z_copy(d).start()

    service0()

    pltpu.make_async_copy(diag, diag, d3r).wait()
    top[...] = diag[z]
    unit = jnp.where(
        lax.broadcasted_iota(jnp.int32, (BLK, BLK), 0) == lax.broadcasted_iota(jnp.int32, (BLK, BLK), 1),
        1.0, 0.0,
    )
    services = (service1, service2, service3, None)
    for k in range(4):
        pair[:, :BLK] = diag[k]
        pair[:, BLK:] = unit
        inverse_factor(pair)
        w = pair[:, BLK:]
        if k == 0:
            pltpu.make_async_copy(off, off, oa_r).wait()
        for i in range(k + 1, 4):
            lower[OFF_AT[i, k]] = product_nt(off[OFF_AT[i, k]], w)
        for i in range(k + 1, 4):
            for j in range(k + 1, i + 1):
                change = product_nt(lower[OFF_AT[i, k]], lower[OFF_AT[j, k]])
                if i == j:
                    diag[i] = diag[i] - change
                else:
                    off[OFF_AT[i, j]] = off[OFF_AT[i, j]] - change
        for j in range(k):
            part = product_nn(lower[OFF_AT[k, j]], inv[j * 4 + j])
            for m in range(j + 1, k):
                part = part + product_nn(lower[OFF_AT[k, m]], inv[m * 4 + j])
            inv[k * 4 + j] = -product_nn(w, part)
        inv[k * 4 + k] = w

        @pl.when(z == k)
        def _():
            for j in range(k + 1):
                vz[j] = inv[k * 4 + j]

        if services[k] is not None:
            services[k]()

    out_ref[...] = product_nt(sall[z], vz[z])
    for d in range(1, 4):
        @pl.when(z >= d)
        def _():
            remote(sall.at[z - d], sall.at[z - d], zs.at[d], zr.at[d], sub, z).wait_recv()
            out_ref[...] += product_nt(sall[z - d], vz[z - d])

    loop(1, 8, d1_copy, "wait_send")
    loop(1, 4, d2_copy, "wait_send")
    loop(1, 32, d3_copy, "wait_send")
    scatter("wait_send")

    @pl.when((holder < 6) & (y == 0))
    def _():
        loop(1, 4, fw_copy, "wait_send")

    @pl.when(holder < 6)
    def _():
        loop(1, 32, oa_copy, "wait_send")

    for r in range(4):
        s0_copy(r).wait_send()
    for kind in range(6):
        for h in range(2):
            s1_copy(kind, h).wait_send()
    for h in range(2):
        for d in range(1, 4):
            s2_copy(h, d).wait_send()
    for d in range(1, 4):
        @pl.when(z + d < 4)
        def _():
            z_copy(d).wait_send()


def panel_solve(first, links, slots, interface_panel):
    blocks = lambda *lead: pltpu.VMEM((*lead, BLK, BLK), F32)
    dma = lambda n: pltpu.SemaphoreType.DMA((n,))
    return pl.pallas_call(
        functools.partial(panel_kernel, 4),
        out_shape=jax.ShapeDtypeStruct(interface_panel.shape, F32),
        in_specs=[
            pl.BlockSpec(memory_space=pltpu.SMEM),
            pl.BlockSpec(memory_space=pltpu.VMEM),
            pl.BlockSpec(memory_space=pltpu.VMEM),
            pl.BlockSpec(memory_space=pltpu.VMEM),
        ],
        out_specs=pl.BlockSpec(memory_space=pltpu.VMEM),
        scratch_shapes=[
            blocks(),
            pltpu.VMEM((8, 16, BLK), F32),
            pltpu.VMEM((4, 16, BLK), F32),
            pltpu.VMEM((16, BLK), F32),
            blocks(4),
            pltpu.VMEM((32, BLK), F32),
            blocks(6),
            blocks(4, 2, 4), blocks(4, 2, 4), blocks(4, 2, 4),
            blocks(2, 2), blocks(2, 2), blocks(2, 2), blocks(2, 2), blocks(2, 2), blocks(2, 2),
            blocks(6),
            pltpu.VMEM((4, 2 * BLK, BLK), F32),
            pltpu.VMEM((BLK, 2 * BLK), F32),
            blocks(6), blocks(16), blocks(4), blocks(),
            dma(8), dma(8), dma(4), dma(4), dma(32), pltpu.SemaphoreType.DMA,
            dma(24), pltpu.SemaphoreType.DMA, dma(4), dma(32), pltpu.SemaphoreType.DMA,
            dma(4), dma(4), dma(12), dma(12), dma(6), dma(6), dma(4), dma(4),
        ],
        compiler_params=pltpu.CompilerParams(
            collective_id=0, has_side_effects=True, vmem_limit_bytes=48 << 20
        ),
        name="panel_solve",
    )(slots, first, links, interface_panel)


def shards(coupling_blocks, block_inverse, coupling_pattern, link_blocks, interface_panel):
    first, links, slots = local_updates(
        coupling_blocks, block_inverse, coupling_pattern, link_blocks, 64
    )
    return panel_solve(first, links, slots, interface_panel)


def solution(mesh):
    in_specs = (
        P(("sub", "blk"), None, None, None, None),
        P(("sub", "blk"), None, None, None),
        P(("sub", "blk"), None, None),
        P(("sub", "blk"), None),
        P("sub", "blk"),
    )
    out_specs = P("sub", "blk")
    return jax.shard_map(shards, mesh=mesh, in_specs=in_specs, out_specs=out_specs, check_vma=False)
```

time: 424 us -> 71.8 us (0.17); the launches traced: 417 us -> 71.6 us
  waiting for transfers between devices: 241 us -> 0 us
  other arithmetic: 99.3 us -> 0 us
  Pallas kernels: 0 us -> 67.9 us
  matrix products: 34.5 us -> 0 us
  between operations: 16.3 us -> 0.03 us
  local copies, waits for them, and re-layouts: 17.7 us -> 3.71 us
  starting transfers between devices: 8.53 us -> 0 us
    psum x1 -> x0, waiting for transfers between devices: 101 us -> none  [shards(): lax.psum(lax.dynamic_update_slice_in_dim(padded, own_rows, offset, 0)[:pa...]
    another operation x17 -> x0, other arithmetic: 88.8 us -> none  [the longest x14 78.8 us: shards(): diag_factor = jnp.linalg.cholesky(diag_block)]
    reduce_scatter x1 -> x0, waiting for transfers between devices: 82.6 us -> none  [shards(): lax.psum_scatter(placed_rows.reshape(row_count * lax.axis_size('sub'), bl...]
    pallas_call x0 -> x2, Pallas kernels: none -> 67.9 us  [the longest x1 46.5 us: panel_solve(): pl.pallas_call(functools.partial(panel_kernel, 4), out_shape=jax.ShapeDty...]
    ppermute x3 -> x0, waiting for transfers between devices: 32.7 us -> none  [passed_along(): return lax.ppermute(block, axis, route)]
    dot_general x6 -> x0, matrix products: 26.6 us -> none  [the longest x1 16.6 us: shards(): updates = jnp.einsum('nclij,ncjk->nlik', masked, solved, precision=HIGHEST)]
    all_gather x1 -> x0, waiting for transfers between devices: 24.7 us -> none  [shards(): diag_block = lax.all_gather(diag_column, 'blk', axis=1, tiled=True)]
    ppermute x3 -> x0, starting transfers between devices: 8.04 us -> none  [passed_along(): return lax.ppermute(block, axis, route)]
  transfers between devices with their start and end apart: 6 -> 0, of which waited for: 6 -> 0; matrix products, arithmetic and copies ran while one was open for 0% -> 0% of each run, Pallas kernels for 0% -> 0%
where the time goes in v1:
time: 71.8 us; the launch traced here: 71.6 us
  Pallas kernels  67.9 us (95%)
  local copies, waits for them, and re-layouts  3.71 us (5%)
    pallas_call x1, Pallas kernels, panel_solve(): pl.pallas_call(functools.partial(panel_kernel, 4), out_shape=jax.ShapeDty...  46.5 us
    pallas_call x1, Pallas kernels, local_updates(): pl.pallas_call(update_kernel, out_shape=(jax.ShapeDtypeStruct((BLK, BLK),...  21.4 us
    unnamed x8, local copies, waits for them, and re-layouts  3.71 us

profile of v1, /device:TPU:64, one launch (start us, length us, event | category | flops | bytes accessed | tf_op | source)
XLA Modules:
  0.0 71.6 jit_solution(14270589817571880277)
XLA Ops:
  0.0 0.8 %copy.6.pattern_ref = s32[2,16,9]{2,1,0:T(8,128)S(1)} copy(s32[2,16,9]{1,0,2:T(2,128)} %param.7) | data formatting | bytes 2304 | tf_op args[2]
  0.8 0.0 copy-start
  0.8 1.6 %copy-done = f32[2,16,128,128]{3,2,1,0:T(8,128)S(1)} copy-done((f32[2,16,128,128]{3,2,1,0:T(8,128)S(1)}, f32[2,16,128,128]{3,2,1,0:T(8,128)}, u32[]{:S(2)}) %copy-start) | copy-done | bytes 2097176
  2.4 0.0 copy-start.2
  2.4 0.7 copy-done.2
  3.1 0.0 copy-start.1
  3.1 21.4 %local_updates.1 = (f32[128,128]{1,0:T(8,128)S(1)}, f32[17,128,128]{2,1,0:T(8,128)S(1)}, s32[2,64]{1,0:T(2,128)S(1)}) custom-call(s32[2,16,9]{2,1,0:T(8,128)S(1)} %copy.6.pattern_ref, s32[2,8]{1,0:T(2,128)S(1)} %copy-done.2, f32[2,16,9,128,128]{4,3,2,1,0:T(8,128)} %coupling_ref.1, f32[2,16,128,128]{3,2,1,0:T(8,128)S(1)} %copy-done), custom_call_target="tpu_custom_call" | custom-call | tf_op jit(solution)/shard_map/local_updates/pallas_call | solution.py:118
  24.5 0.0 copy-done.1
  24.5 46.5 %panel_solve.1 = f32[256,128]{1,0:T(8,128)S(1)} custom-call(s32[2,64]{1,0:T(2,128)S(1)} %get-tuple-element.8.slot_ref, f32[128,128]{1,0:T(8,128)S(1)} %get-tuple-element.9.first_ref, f32[17,128,128]{2,1,0:T(8,128)S(1)} %get-tuple-element.10.links_ref, f32[256,128]{1,0:T(8,128)S(1)} %copy-done.1), custom_call_target="tpu_custom_call" | custom-call | tf_op jit(solution)/shard_map/panel_solve/pallas_call | solution.py:499
  71.0 0.7 copy.8
Async XLA Ops:
  0.8 1.6 %copy-start = (f32[2,16,128,128]{3,2,1,0:T(8,128)S(1)}, f32[2,16,128,128]{3,2,1,0:T(8,128)}, u32[]{:S(2)}) copy-start(f32[2,16,128,128]{3,2,1,0:T(8,128)} %inverse_ref.1) | copy-start | bytes 6291460
  2.4 0.7 copy-start.2
  3.1 21.4 %copy-start.1 = (f32[256,128]{1,0:T(8,128)S(1)}, f32[256,128]{1,0:T(8,128)}, u32[]{:S(2)}) copy-start(f32[256,128]{1,0:T(8,128)} %panel_ref.1) | copy-start | bytes 393220

commit v2 on v1

--- a/solution.py
+++ b/solution.py
@@ -11,7 +11,7 @@
 BF16 = jnp.bfloat16
 MESH = pl.DeviceIdType.MESH
 BLK = 128
-CHUNK = 4
+GROUP = 8
 STEP = 16
 OFF = ((1, 0), (2, 0), (3, 0), (2, 1), (3, 1), (3, 2))
 OFF_AT = {pair: k for k, pair in enumerate(OFF)}
@@ -43,111 +43,7 @@
     )
 
 
-def update_kernel(
-    pattern_ref, link_ref, coupling_ref, inverse_ref,
-    first_ref, links_ref, slot_ref,
-    cbuf, ibuf, lhs, rhs, acc, csem, isem,
-):
-    subs, cells = coupling_ref.shape[0], coupling_ref.shape[1]
-    faces = coupling_ref.shape[2]
-    links = faces - 1
-    none = subs * links
-    rows = faces * BLK
-
-    def fetch(i, carry):
-        n, c = i // cells, lax.rem(i, cells)
-        pltpu.make_async_copy(inverse_ref.at[n, c], ibuf.at[i], isem.at[i]).start()
-        pltpu.make_async_copy(coupling_ref.at[n, c], cbuf.at[i], csem.at[i]).start()
-        return carry
-
-    lax.fori_loop(0, subs * cells, fetch, 0)
-
-    def clear(i, carry):
-        for n in range(subs):
-            slot_ref[n, i] = none
-        return carry
-
-    lax.fori_loop(0, slot_ref.shape[1], clear, 0)
-    for n in range(subs):
-        for l in range(links):
-            slot_ref[n, link_ref[n, l]] = n * links + l
-    links_ref[none] = jnp.zeros((BLK, BLK), F32)
-
-    for n in range(subs):
-        def chunk_step(chunk, carry):
-            for k in range(CHUNK):
-                cell = chunk * CHUNK + k
-                i = n * cells + cell
-                pltpu.make_async_copy(inverse_ref.at[n, cell], ibuf.at[i], isem.at[i]).wait()
-                pltpu.make_async_copy(coupling_ref.at[n, cell], cbuf.at[i], csem.at[i]).wait()
-                for l in range(faces):
-                    block = cbuf[i, l] * pattern_ref[n, cell, l].astype(F32)
-                    high, low = halves(block)
-                    if l == 0:
-                        solved = product_nt(ibuf[i], block)
-                    place = pl.ds(l * BLK, BLK)
-                    lhs[place, pl.ds(k * 2 * BLK, BLK)] = high
-                    lhs[place, pl.ds(k * 2 * BLK + BLK, BLK)] = low
-                sh, sl = halves(solved)
-                rhs[pl.ds(k * 2 * BLK, BLK), :] = jnp.concatenate([sh, sl], axis=1)
-                rhs[pl.ds(k * 2 * BLK + BLK, BLK), :] = jnp.concatenate([sh, jnp.zeros_like(sl)], axis=1)
-            part = jnp.dot(lhs[...], rhs[...], preferred_element_type=F32)
-
-            @pl.when(chunk == 0)
-            def _():
-                acc[...] = part
-
-            @pl.when(chunk > 0)
-            def _():
-                acc[...] += part
-
-            return carry
-
-        lax.fori_loop(0, cells // CHUNK, chunk_step, 0)
-        total = acc[:, :BLK] + acc[:, BLK:]
-        if n == 0:
-            first_ref[...] = total[:BLK]
-        else:
-            first_ref[...] += total[:BLK]
-        links_ref[n * links : (n + 1) * links] = total[BLK:].reshape(links, BLK, BLK)
-
-
-def local_updates(coupling_blocks, block_inverse, coupling_pattern, link_blocks, block_rows):
-    subs, cells, faces = coupling_blocks.shape[:3]
-    rows = faces * BLK
-    return pl.pallas_call(
-        update_kernel,
-        out_shape=(
-            jax.ShapeDtypeStruct((BLK, BLK), F32),
-            jax.ShapeDtypeStruct((subs * (faces - 1) + 1, BLK, BLK), F32),
-            jax.ShapeDtypeStruct((subs, block_rows), jnp.int32),
-        ),
-        in_specs=[
-            pl.BlockSpec(memory_space=pltpu.SMEM),
-            pl.BlockSpec(memory_space=pltpu.SMEM),
-            pl.BlockSpec(memory_space=pl.ANY),
-            pl.BlockSpec(memory_space=pl.ANY),
-        ],
-        out_specs=(
-            pl.BlockSpec(memory_space=pltpu.VMEM),
-            pl.BlockSpec(memory_space=pltpu.VMEM),
-            pl.BlockSpec(memory_space=pltpu.SMEM),
-        ),
-        scratch_shapes=[
-            pltpu.VMEM((subs * cells, faces, BLK, BLK), F32),
-            pltpu.VMEM((subs * cells, BLK, BLK), F32),
-            pltpu.VMEM((rows, CHUNK * 2 * BLK), BF16),
-            pltpu.VMEM((CHUNK * 2 * BLK, 2 * BLK), BF16),
-            pltpu.VMEM((rows, 2 * BLK), F32),
-            pltpu.SemaphoreType.DMA((subs * cells,)),
-            pltpu.SemaphoreType.DMA((subs * cells,)),
-        ],
-        compiler_params=pltpu.CompilerParams(vmem_limit_bytes=48 << 20),
-        name="local_updates",
-    )(coupling_pattern, link_blocks, coupling_blocks, block_inverse)
-
-
-def inverse_factor(pair):
+def inverse_factor(pair, between):
     rows = lax.broadcasted_iota(jnp.int32, (STEP, BLK), 0)
     for r in range(0, BLK, STEP):
         pa, pe = pair[r : r + STEP, :BLK], pair[r : r + STEP, BLK:]
@@ -171,10 +67,12 @@
                 preferred_element_type=F32,
             )
             pair[r + STEP :, :] = pair[r + STEP :, :] - change[r + STEP :, :]
+        between(r // STEP)
 
 
 def panel_kernel(
-    nx, slot_ref, first_ref, links_ref, panel_ref, out_ref,
+    nx, pattern_ref, link_ref, coupling_ref, inverse_ref, interface_ref, out_ref,
+    pattern, link, panel_ref, firsts, faces, inverses, rhs, links_ref, small_s, inv_s, first_s, face_s,
     firstc, gather1, gather2, piece, diag, offpiece, off,
     send0, recv0, acc, relay_r, relay_l, direct_r, direct_l, onward_r, onward_l,
     last, sall, pair, lower, inv, vz, top,
@@ -219,7 +117,74 @@
 
     lax.fori_loop(1, 4, greet_y, 0)
 
-    firstc[...] = -first_ref[...]
+    subs, cells, links = coupling_ref.shape[0], coupling_ref.shape[1], coupling_ref.shape[2] - 1
+    per_sub = cells // GROUP
+    none = subs * links
+    small = [
+        pltpu.make_async_copy(pattern_ref, pattern, small_s.at[0]),
+        pltpu.make_async_copy(link_ref, link, small_s.at[1]),
+        pltpu.make_async_copy(interface_ref, panel_ref, small_s.at[2]),
+    ]
+    inv_in, first_in, face_in = [], [], []
+    for g in range(subs * per_sub):
+        n, c = g // per_sub, pl.ds(g % per_sub * GROUP, GROUP)
+        held = pl.ds(g * GROUP, GROUP)
+        inv_in.append(pltpu.make_async_copy(inverse_ref.at[n, c], inverses.at[held], inv_s.at[g]))
+        first_in.append(pltpu.make_async_copy(coupling_ref.at[n, c, 0], firsts.at[held], first_s.at[g]))
+        face_in.append(
+            pltpu.make_async_copy(coupling_ref.at[n, c, pl.ds(1, links)], faces.at[held], face_s.at[g])
+        )
+    for copy in small + [copy for both in zip(inv_in, first_in) for copy in both] + face_in:
+        copy.start()
+    links_ref[none] = jnp.zeros((BLK, BLK), F32)
+
+    zero = jnp.zeros((BLK, BLK), BF16)
+    small[0].wait()
+    for g in range(subs * per_sub):
+        inv_in[g].wait()
+        first_in[g].wait()
+        left, right = [], []
+        for i in range(g * GROUP, g * GROUP + GROUP):
+            bh, bl = halves(firsts[i] * pattern[0, i // cells, i % cells].astype(F32))
+            ih, il = halves(inverses[i])
+            weight = jnp.concatenate(
+                [jnp.concatenate([bh, bh], axis=1), jnp.concatenate([bl, zero], axis=1)], axis=0
+            )
+            both = lax.dot_general(
+                jnp.concatenate([ih, il], axis=1), weight, (((1,), (1,)), ((), ())),
+                preferred_element_type=F32,
+            )
+            sh, sl = halves(both[:, :BLK] + both[:, BLK:])
+            pair_hl = jnp.concatenate([sh, sl], axis=1)
+            rhs[i] = pair_hl
+            left += [bh, bl]
+            right += [pair_hl, jnp.concatenate([sh, zero], axis=1)]
+        both = jnp.dot(
+            jnp.concatenate(left, axis=1), jnp.concatenate(right, axis=0), preferred_element_type=F32
+        )
+        part = both[:, :BLK] + both[:, BLK:]
+        firstc[...] = -part if g == 0 else firstc[...] - part
+
+    def link_updates(g):
+        face_in[g].wait()
+        n = g // per_sub
+        highs, lows = [], []
+        for i in range(g * GROUP, g * GROUP + GROUP):
+            value = jnp.concatenate(
+                [faces[i, l] * pattern[l + 1, n, i % cells].astype(F32) for l in range(links)], axis=0
+            )
+            high, low = halves(value)
+            highs.append(high)
+            lows.append(low)
+        right = rhs[g * GROUP : (g + 1) * GROUP].reshape(GROUP * BLK, 2 * BLK)
+        both = jnp.dot(jnp.concatenate(highs, axis=1), right, preferred_element_type=F32)
+        rest = jnp.dot(jnp.concatenate(lows, axis=1), right[:, :BLK], preferred_element_type=F32)
+        part = (both[:, :BLK] + both[:, BLK:] + rest).reshape(links, BLK, BLK)
+        held = pl.ds(n * links, links)
+        links_ref[held] = part if g % per_sub == 0 else links_ref[held] + part
+
+    small[1].wait()
+    small[2].wait()
 
     @pl.when(sub == z // 2)
     def _():
@@ -278,11 +243,60 @@
 
     scatter("start")
 
+    link_updates(0)
+    loop(1, 8, d1_copy, "wait_recv")
+    gather2[y] = jnp.sum(gather1[...], axis=0)
+    loop(1, 4, d2_copy, "start")
+
+    link_updates(1)
+
+    holder = z * 2 + core
+
+    def fw_copy(t):
+        return remote(offpiece, offpiece, fw_s.at[t], op_r, sub_of(lax.rem(y + t, 4), x, core), z)
+
+    @pl.when(holder < 6)
+    def _():
+        pltpu.make_async_copy(offpiece, offpiece, op_r).wait()
+
+    @pl.when((holder < 6) & (y == 0))
+    def _():
+        loop(1, 4, fw_copy, "start")
+
+    loop(1, 4, d2_copy, "wait_recv")
+    piece[...] = jnp.sum(gather2[...], axis=0)
+    own_diag = pltpu.make_async_copy(piece, diag.at[z, mine], d3r)
+    own_diag.start()
+    loop(1, 32, d3_copy, "start")
+
+    link_updates(2)
+
+    quarter = pl.ds(pl.multiple_of(x * 32, 32), 32)
+
+    def oa_copy(t):
+        to_sub, to_z = plane_peer(t)
+        return remote(offpiece, off.at[holder, quarter], oa_s.at[t], oa_r, to_sub, to_z)
+
+    @pl.when(holder < 6)
+    def _():
+        pltpu.make_async_copy(offpiece, off.at[holder, quarter], oa_r).start()
+        loop(1, 32, oa_copy, "start")
+
+    link_updates(3)
+
+    names = [[link[n, l] for l in range(links)] for n in range(subs)]
+
+    def slot(n, g):
+        found = jnp.int32(none)
+        for l in range(links):
+            found = jnp.where(names[n][l] == g, n * links + l, found)
+        return found
+
     def placed(r, h, other, to_core):
         to_x = lax.rem(x + r, 4) if h == 0 else other
         to_y = other if h == 0 else lax.rem(y + r, 4)
         g = sub_of(to_y, to_x, to_core) * 2 + h
-        return links_ref[slot_ref[0, g]] + links_ref[slot_ref[1, g]]
+        return links_ref[slot(0, g)] + links_ref[slot(1, g)]
 
     def fill(ref, r, to_core):
         def body(other, carry):
@@ -295,47 +309,9 @@
     def s0_copy(r):
         return remote(send0.at[r], recv0.at[r], s0s.at[r], s0r.at[r], sub_of(y, x, 1 - core), z)
 
-    for r in (2, 1):
+    for r in (2, 1, 3, 0):
         fill(send0, r, 1 - core)
         s0_copy(r).start()
-
-    loop(1, 8, d1_copy, "wait_recv")
-    gather2[y] = jnp.sum(gather1[...], axis=0)
-    loop(1, 4, d2_copy, "start")
-
-    for r in (3, 0):
-        fill(send0, r, 1 - core)
-        s0_copy(r).start()
-
-    holder = z * 2 + core
-
-    def fw_copy(t):
-        return remote(offpiece, offpiece, fw_s.at[t], op_r, sub_of(lax.rem(y + t, 4), x, core), z)
-
-    @pl.when(holder < 6)
-    def _():
-        pltpu.make_async_copy(offpiece, offpiece, op_r).wait()
-
-    @pl.when((holder < 6) & (y == 0))
-    def _():
-        loop(1, 4, fw_copy, "start")
-
-    loop(1, 4, d2_copy, "wait_recv")
-    piece[...] = jnp.sum(gather2[...], axis=0)
-    own_diag = pltpu.make_async_copy(piece, diag.at[z, mine], d3r)
-    own_diag.start()
-    loop(1, 32, d3_copy, "start")
-
-    quarter = pl.ds(pl.multiple_of(x * 32, 32), 32)
-
-    def oa_copy(t):
-        to_sub, to_z = plane_peer(t)
-        return remote(offpiece, off.at[holder, quarter], oa_s.at[t], oa_r, to_sub, to_z)
-
-    @pl.when(holder < 6)
-    def _():
-        pltpu.make_async_copy(offpiece, off.at[holder, quarter], oa_r).start()
-        loop(1, 32, oa_copy, "start")
 
     def ring(h, step):
         if h == 0:
@@ -359,18 +335,12 @@
         s0_copy(r).wait_recv()
         acc[r] += recv0[r]
 
-    def service0():
-        arrive0(2)
-        for h in range(2):
-            s1_copy(0, h).start()
-            s1_copy(1, h).start()
-        arrive0(1)
-        for h in range(2):
-            s1_copy(2, h).start()
-        arrive0(3)
-        for h in range(2):
-            s1_copy(3, h).start()
-        arrive0(0)
+    def service0(r):
+        arrive0(r)
+        if r:
+            for kind in {2: (0, 1), 1: (2,), 3: (3,)}[r]:
+                for h in range(2):
+                    s1_copy(kind, h).start()
 
     def service1():
         for h in range(2):
@@ -419,19 +389,25 @@
             def _():
                 z_copy(d).start()
 
-    service0()
-
     pltpu.make_async_copy(diag, diag, d3r).wait()
     top[...] = diag[z]
     unit = jnp.where(
         lax.broadcasted_iota(jnp.int32, (BLK, BLK), 0) == lax.broadcasted_iota(jnp.int32, (BLK, BLK), 1),
         1.0, 0.0,
     )
-    services = (service1, service2, service3, None)
+    hooks = {
+        (0, 1): lambda: service0(2),
+        (0, 3): lambda: service0(1),
+        (0, 5): lambda: service0(3),
+        (0, 7): lambda: service0(0),
+        (1, 3): service1,
+        (2, 5): service2,
+        (3, 2): service3,
+    }
     for k in range(4):
         pair[:, :BLK] = diag[k]
         pair[:, BLK:] = unit
-        inverse_factor(pair)
+        inverse_factor(pair, lambda r, k=k: hooks.get((k, r), lambda: None)())
         w = pair[:, BLK:]
         if k == 0:
             pltpu.make_async_copy(off, off, oa_r).wait()
@@ -456,9 +432,6 @@
             for j in range(k + 1):
                 vz[j] = inv[k * 4 + j]
 
-        if services[k] is not None:
-            services[k]()
-
     out_ref[...] = product_nt(sall[z], vz[z])
     for d in range(1, 4):
         @pl.when(z >= d)
@@ -493,20 +466,26 @@
             z_copy(d).wait_send()
 
 
-def panel_solve(first, links, slots, interface_panel):
+def panel_solve(pattern, link, coupling, inverse, interface):
+    subs, cells, faces = coupling.shape[:3]
     blocks = lambda *lead: pltpu.VMEM((*lead, BLK, BLK), F32)
     dma = lambda n: pltpu.SemaphoreType.DMA((n,))
+    groups = subs * cells // GROUP
     return pl.pallas_call(
         functools.partial(panel_kernel, 4),
-        out_shape=jax.ShapeDtypeStruct(interface_panel.shape, F32),
-        in_specs=[
-            pl.BlockSpec(memory_space=pltpu.SMEM),
-            pl.BlockSpec(memory_space=pltpu.VMEM),
-            pl.BlockSpec(memory_space=pltpu.VMEM),
-            pl.BlockSpec(memory_space=pltpu.VMEM),
-        ],
+        out_shape=jax.ShapeDtypeStruct(interface.shape, F32),
+        in_specs=[pl.BlockSpec(memory_space=pltpu.HBM)] * 5,
         out_specs=pl.BlockSpec(memory_space=pltpu.VMEM),
         scratch_shapes=[
+            pltpu.SMEM(pattern.shape, jnp.int32),
+            pltpu.SMEM(link.shape, jnp.int32),
+            pltpu.VMEM(interface.shape, F32),
+            blocks(subs * cells),
+            blocks(subs * cells, faces - 1),
+            blocks(subs * cells),
+            pltpu.VMEM((subs * cells, BLK, 2 * BLK), BF16),
+            blocks(subs * (faces - 1) + 1),
+            dma(3), dma(groups), dma(groups), dma(groups),
             blocks(),
             pltpu.VMEM((8, 16, BLK), F32),
             pltpu.VMEM((4, 16, BLK), F32),
@@ -525,17 +504,15 @@
             dma(4), dma(4), dma(12), dma(12), dma(6), dma(6), dma(4), dma(4),
         ],
         compiler_params=pltpu.CompilerParams(
-            collective_id=0, has_side_effects=True, vmem_limit_bytes=48 << 20
+            collective_id=0, has_side_effects=True, vmem_limit_bytes=60 << 20
         ),
         name="panel_solve",
-    )(slots, first, links, interface_panel)
+    )(pattern, link, coupling, inverse, interface)
 
 
 def shards(coupling_blocks, block_inverse, coupling_pattern, link_blocks, interface_panel):
-    first, links, slots = local_updates(
-        coupling_blocks, block_inverse, coupling_pattern, link_blocks, 64
-    )
-    return panel_solve(first, links, slots, interface_panel)
+    pattern = coupling_pattern.transpose(2, 0, 1)
+    return panel_solve(pattern, link_blocks, coupling_blocks, block_inverse, interface_panel)
 
 
 def solution(mesh):

time: 71.8 us -> 54.3 us (0.76)
  Pallas kernels: 67.9 us -> 52.6 us
  local copies, waits for them, and re-layouts: 3.71 us -> 1.57 us
    pallas_call x1 -> x0, Pallas kernels: 21.4 us -> none  [local_updates(): pl.pallas_call(update_kernel, out_shape=(jax.ShapeDtypeStruct((BLK, BLK),...]
    pallas_call x1, Pallas kernels: 46.5 us -> 52.6 us  [panel_solve(): pl.pallas_call(functools.partial(panel_kernel, 4), out_shape=jax.ShapeDty...]
    unnamed x8 -> x1, local copies, waits for them, and re-layouts: 3.71 us -> 1.57 us
where the time goes in v2:
time: 54.3 us; the launch traced here: 54.2 us
  Pallas kernels  52.6 us (97%)
  local copies, waits for them, and re-layouts  1.57 us (3%)
    pallas_call x1, Pallas kernels, panel_solve(): pl.pallas_call(functools.partial(panel_kernel, 4), out_shape=jax.ShapeDty...  52.6 us
    unnamed x1, local copies, waits for them, and re-layouts  1.57 us

profile of v2, /device:TPU:64, one launch (start us, length us, event | category | flops | bytes accessed | tf_op | source)
XLA Modules:
  0.0 54.2 jit_solution(6616881163872744689)
XLA Ops:
  0.0 52.6 %panel_solve.1 = f32[256,128]{1,0:T(8,128)} custom-call(s32[9,2,16]{2,1,0:T(2,128)} %bitcast.1, s32[2,8]{1,0:T(2,128)} %link_ref.1, f32[2,16,9,128,128]{4,3,2,1,0:T(8,128)} %coupling_ref.1, f32[2,16,128,128]{3,2,1,0:T(8,128)} %inverse_ref.1, f32[256,128]{1,0:T(8,128)} %interface_ref.1), custom_call_target="tpu_custom_call" | custom-call | tf_op jit(solution)/shard_map/panel_solve/pallas_call | solution.py:474
  52.6 1.6 %copy.7 = f32[256,128]{1,0:T(8,128)} copy(f32[256,128]{1,0:T(8,128)} %panel_solve.1) | data formatting | bytes 262144

commit v3 on v2

--- a/solution.py
+++ b/solution.py
@@ -72,11 +72,12 @@
 
 def panel_kernel(
     nx, pattern_ref, link_ref, coupling_ref, inverse_ref, interface_ref, out_ref,
-    pattern, link, panel_ref, firsts, faces, inverses, rhs, links_ref, small_s, inv_s, first_s, face_s,
-    firstc, gather1, gather2, piece, diag, offpiece, off,
-    send0, recv0, acc, relay_r, relay_l, direct_r, direct_l, onward_r, onward_l,
+    pattern, link, peer_link, panel_ref, firsts, faces, inverses, rhs, links_ref, peer_links,
+    small_s, inv_s, first_s, face_s,
+    firstc, gather1, gather2, pieces, top_cols,
+    acc, relay_r, relay_l, direct_r, direct_l, onward_r, onward_l,
     last, sall, pair, lower, inv, vz, top,
-    d1s, d1r, d2s, d2r, d3s, d3r, sc_s, op_r, fw_s, oa_s, oa_r,
+    d1s, d1r, d2s, d2r, d3s, d3r, sc_s, op_r, fw_s,
     s0s, s0r, s1s, s1r, s2s, s2r, zs, zr,
 ):
     sub, z = lax.axis_index("sub"), lax.axis_index("blk")
@@ -93,29 +94,25 @@
             device_id=(to_sub, to_z), device_id_type=MESH,
         )
 
-    place = (core * 4 + x) * 4 + z
-
-    def plane_peer(t):
-        e = lax.rem(place + t, 32)
-        q = e // 4
-        return sub_of(y, lax.rem(q, 4), q // 4), lax.rem(e, 4)
+    q = core * 4 + x
+
+    def row_peer(t):
+        to = lax.rem(q + t, 8)
+        return to, sub_of(y, lax.rem(to, 4), to // 4)
+
+    def y_peer(t):
+        return sub_of(lax.rem(y + t, 4), x, core)
 
     barrier = pltpu.get_barrier_semaphore()
 
-    def greet(t, carry):
-        to_sub, to_z = plane_peer(t)
+    def greet(to_sub, to_z):
         pl.semaphore_signal(barrier, inc=1, device_id=(to_sub, to_z), device_id_type=MESH)
-        return carry
-
-    lax.fori_loop(1, 32, greet, 0)
-
-    def greet_y(t, carry):
-        pl.semaphore_signal(
-            barrier, inc=1, device_id=(sub_of(lax.rem(y + t, 4), x, core), z), device_id_type=MESH
-        )
-        return carry
-
-    lax.fori_loop(1, 4, greet_y, 0)
+
+    for t in range(1, 8):
+        greet(row_peer(t)[1], z)
+    for t in range(1, 4):
+        greet(y_peer(t), z)
+        greet(sub, lax.rem(z + t, 4))
 
     subs, cells, links = coupling_ref.shape[0], coupling_ref.shape[1], coupling_ref.shape[2] - 1
     per_sub = cells // GROUP
@@ -137,6 +134,7 @@
     for copy in small + [copy for both in zip(inv_in, first_in) for copy in both] + face_in:
         copy.start()
     links_ref[none] = jnp.zeros((BLK, BLK), F32)
+    peer_links[none] = jnp.zeros((BLK, BLK), F32)
 
     zero = jnp.zeros((BLK, BLK), BF16)
     small[0].wait()
@@ -188,130 +186,122 @@
 
     @pl.when(sub == z // 2)
     def _():
-        firstc[...] += panel_ref[pl.ds(pl.multiple_of(lax.rem(z, 2) * BLK, BLK), BLK), :]
-
-    pl.semaphore_wait(barrier, 34)
-
-    q = core * 4 + x
-
-    def d1_copy(t):
-        to = lax.rem(q + t, 8)
-        return remote(
-            firstc.at[pl.ds(pl.multiple_of(to * 16, 16), 16)], gather1.at[q],
-            d1s.at[t], d1r.at[t], sub_of(y, lax.rem(to, 4), to // 4), z,
-        )
-
-    def d2_copy(t):
-        return remote(
-            gather2.at[y], gather2.at[y], d2s.at[t], d2r.at[t],
-            sub_of(lax.rem(y + t, 4), x, core), z,
-        )
+        firstc[...] += panel_ref[lax.rem(z, 2)]
+
+    pl.semaphore_wait(barrier, 13)
 
     mine = pl.ds(pl.multiple_of(q * 16, 16), 16)
 
-    def d3_copy(t):
-        to_sub, to_z = plane_peer(t)
-        return remote(piece, diag.at[z, mine], d3s.at[t], d3r, to_sub, to_z)
-
-    def loop(low, high, make, *actions):
-        def body(t, carry):
-            copy = make(t)
-            for action in actions:
-                getattr(copy, action)()
-            return carry
-
-        lax.fori_loop(low, high, body, 0)
-
-    loop(1, 8, d1_copy, "start")
+    def landed(ref, sem):
+        pltpu.make_async_copy(ref, ref, sem).wait()
+
+    for t in range(1, 8):
+        to, to_sub = row_peer(t)
+        remote(
+            firstc.at[pl.ds(pl.multiple_of(to * 16, 16), 16)], gather1.at[q], d1s, d1r, to_sub, z
+        ).start()
     gather1[q] = firstc[mine, :]
 
-    def scatter(action):
-        for k, (i, j) in enumerate(OFF):
-            @pl.when((sub == i // 2) & (z == j))
-            def _(k=k, i=i, j=j):
-                for xx in range(4):
-                    src = panel_ref.at[pl.ds((i % 2) * BLK + xx * 32, 32)]
-                    if xx == 0 and k % 2 == i // 2 and k // 2 == j:
-                        if action == "start":
-                            pltpu.make_async_copy(src, offpiece, op_r).start()
-                    else:
-                        copy = remote(
-                            src, offpiece, sc_s.at[k * 4 + xx], op_r,
-                            jnp.int32(xx * 2 + k % 2), jnp.int32(k // 2),
-                        )
-                        getattr(copy, action)()
-
-    scatter("start")
+    SOURCES = ((0, 0, 1, 2), (1, 0, 0, 2), (1, 1, 0, 2), (1, 2, 1, 2))
+
+    def source_copy(t, owner, low, high):
+        to, to_sub = row_peer(t)
+        src = panel_ref.at[low:high, pl.ds(pl.multiple_of(to * 16, 16), 16)]
+        dst = pieces.at[2 * owner + low : 2 * owner + high]
+        if t == 0:
+            return pltpu.make_async_copy(src, dst, op_r)
+        return remote(src, dst, sc_s, op_r, to_sub, z)
+
+    for owner, column, low, high in SOURCES:
+        @pl.when((sub == owner) & (z == column))
+        def _(owner=owner, low=low, high=high):
+            for t in range(8):
+                source_copy(t, owner, low, high).start()
+
+    peer = sub_of(y, x, 1 - core)
+    link_copy = remote(link, peer_link, s0s.at[2], s0r.at[2], peer, z)
+    link_copy.start()
+
+    def s0_copy(n):
+        part = pl.ds(n * links, links)
+        return remote(links_ref.at[part], peer_links.at[part], s0s.at[n], s0r.at[n], peer, z)
+
+    def fw_copy(t, column):
+        part = pieces.at[column + 1 : 4]
+        return remote(part, part, fw_s.at[t], op_r, y_peer(t), z)
 
     link_updates(0)
-    loop(1, 8, d1_copy, "wait_recv")
+    link_updates(1)
+    s0_copy(0).start()
+
+    landed(gather1.at[0:7], d1r)
     gather2[y] = jnp.sum(gather1[...], axis=0)
-    loop(1, 4, d2_copy, "start")
-
-    link_updates(1)
-
-    holder = z * 2 + core
-
-    def fw_copy(t):
-        return remote(offpiece, offpiece, fw_s.at[t], op_r, sub_of(lax.rem(y + t, 4), x, core), z)
-
-    @pl.when(holder < 6)
-    def _():
-        pltpu.make_async_copy(offpiece, offpiece, op_r).wait()
-
-    @pl.when((holder < 6) & (y == 0))
-    def _():
-        loop(1, 4, fw_copy, "start")
-
-    loop(1, 4, d2_copy, "wait_recv")
-    piece[...] = jnp.sum(gather2[...], axis=0)
-    own_diag = pltpu.make_async_copy(piece, diag.at[z, mine], d3r)
-    own_diag.start()
-    loop(1, 32, d3_copy, "start")
+    for t in range(1, 4):
+        remote(gather2.at[y], gather2.at[y], d2s, d2r, y_peer(t), z).start()
+    for column in range(3):
+        @pl.when((z == column) & (y == 0))
+        def _(column=column):
+            landed(pieces.at[column + 1 : 4], op_r)
+            for t in range(1, 4):
+                fw_copy(t, column).start()
 
     link_updates(2)
-
-    quarter = pl.ds(pl.multiple_of(x * 32, 32), 32)
-
-    def oa_copy(t):
-        to_sub, to_z = plane_peer(t)
-        return remote(offpiece, off.at[holder, quarter], oa_s.at[t], oa_r, to_sub, to_z)
-
-    @pl.when(holder < 6)
-    def _():
-        pltpu.make_async_copy(offpiece, off.at[holder, quarter], oa_r).start()
-        loop(1, 32, oa_copy, "start")
-
     link_updates(3)
-
+    s0_copy(1).start()
+
+    landed(gather2.at[0:3], d2r)
+    pieces[z] = jnp.sum(gather2[...], axis=0)
+    for column in range(3):
+        @pl.when((z == column) & (y > 0))
+        def _(column=column):
+            landed(pieces.at[column + 1 : 4], op_r)
+
+    pltpu.make_async_copy(pieces.at[z], top_cols.at[z, z, mine], d3r.at[z]).start()
+    for ahead in range(3, -1, -1):
+        @pl.when(z + ahead < 4)
+        def _(ahead=ahead):
+            part = pl.ds(z, ahead + 1)
+
+            def send(t, carry):
+                remote(
+                    pieces.at[part], top_cols.at[z, part, mine], d3s.at[ahead], d3r.at[z],
+                    row_peer(t)[1], z + ahead,
+                ).start()
+                return carry
+
+            lax.fori_loop(0 if ahead else 1, 8, send, 0)
+
+    def column_arrives(j):
+        for row in range(j, 4):
+            @pl.when(z == row)
+            def _(row=row):
+                landed(top_cols.at[j, j : row + 1], d3r.at[j])
+
+    link_copy.wait_recv()
     names = [[link[n, l] for l in range(links)] for n in range(subs)]
-
-    def slot(n, g):
+    peer_names = [[peer_link[n, l] for l in range(links)] for n in range(subs)]
+
+    def slot(names, n, g):
         found = jnp.int32(none)
         for l in range(links):
             found = jnp.where(names[n][l] == g, n * links + l, found)
         return found
 
-    def placed(r, h, other, to_core):
-        to_x = lax.rem(x + r, 4) if h == 0 else other
-        to_y = other if h == 0 else lax.rem(y + r, 4)
-        g = sub_of(to_y, to_x, to_core) * 2 + h
-        return links_ref[slot(0, g)] + links_ref[slot(1, g)]
-
-    def fill(ref, r, to_core):
+    def fill(r):
         def body(other, carry):
             for h in range(2):
-                ref[r, h, other] = placed(r, h, other, to_core)
+                to_x = lax.rem(x + r, 4) if h == 0 else other
+                to_y = other if h == 0 else lax.rem(y + r, 4)
+                g = sub_of(to_y, to_x, core) * 2 + h
+                total = links_ref[slot(names, 0, g)]
+                for n in range(1, subs):
+                    total = total + links_ref[slot(names, n, g)]
+                for n in range(subs):
+                    total = total + peer_links[slot(peer_names, n, g)]
+                acc[r, h, other] = total
             return carry
 
         lax.fori_loop(0, 4, body, 0)
-
-    def s0_copy(r):
-        return remote(send0.at[r], recv0.at[r], s0s.at[r], s0r.at[r], sub_of(y, x, 1 - core), z)
-
-    for r in (2, 1, 3, 0):
-        fill(send0, r, 1 - core)
-        s0_copy(r).start()
 
     def ring(h, step):
         if h == 0:
@@ -330,17 +320,13 @@
         )[kind]
         return remote(src, dst, s1s.at[n], s1r.at[n], ring(h, step), z)
 
-    def arrive0(r):
-        fill(acc, r, core)
-        s0_copy(r).wait_recv()
-        acc[r] += recv0[r]
-
-    def service0(r):
-        arrive0(r)
-        if r:
-            for kind in {2: (0, 1), 1: (2,), 3: (3,)}[r]:
-                for h in range(2):
-                    s1_copy(kind, h).start()
+    for n in range(subs):
+        s0_copy(n).wait_recv()
+    for r, kinds in ((2, (0, 1)), (1, (2,)), (3, (3,)), (0, ())):
+        fill(r)
+        for kind in kinds:
+            for h in range(2):
+                s1_copy(kind, h).start()
 
     def service1():
         for h in range(2):
@@ -377,7 +363,7 @@
             for d in range(1, 4):
                 s2_copy(h, d).wait_recv()
                 total = total + last[h * 3 + d - 1]
-            rows = panel_ref[h * BLK : (h + 1) * BLK, :] - total
+            rows = panel_ref[h] - total
             sall[z, h * BLK : (h + 1) * BLK] = rows
 
             @pl.when(sub * 2 + h == z)
@@ -389,37 +375,31 @@
             def _():
                 z_copy(d).start()
 
-    pltpu.make_async_copy(diag, diag, d3r).wait()
-    top[...] = diag[z]
+    column_arrives(0)
     unit = jnp.where(
         lax.broadcasted_iota(jnp.int32, (BLK, BLK), 0) == lax.broadcasted_iota(jnp.int32, (BLK, BLK), 1),
         1.0, 0.0,
     )
     hooks = {
-        (0, 1): lambda: service0(2),
-        (0, 3): lambda: service0(1),
-        (0, 5): lambda: service0(3),
-        (0, 7): lambda: service0(0),
-        (1, 3): service1,
-        (2, 5): service2,
-        (3, 2): service3,
+        (0, 3): service1,
+        (1, 3): service2,
+        (2, 4): service3,
     }
     for k in range(4):
-        pair[:, :BLK] = diag[k]
+        pair[:, :BLK] = top_cols[k, k]
         pair[:, BLK:] = unit
         inverse_factor(pair, lambda r, k=k: hooks.get((k, r), lambda: None)())
         w = pair[:, BLK:]
         if k == 0:
-            pltpu.make_async_copy(off, off, oa_r).wait()
+            for j in range(1, 4):
+                column_arrives(j)
+            top[...] = top_cols[z, z]
         for i in range(k + 1, 4):
-            lower[OFF_AT[i, k]] = product_nt(off[OFF_AT[i, k]], w)
+            lower[OFF_AT[i, k]] = product_nt(top_cols[k, i], w)
         for i in range(k + 1, 4):
             for j in range(k + 1, i + 1):
                 change = product_nt(lower[OFF_AT[i, k]], lower[OFF_AT[j, k]])
-                if i == j:
-                    diag[i] = diag[i] - change
-                else:
-                    off[OFF_AT[i, j]] = off[OFF_AT[i, j]] - change
+                top_cols[j, i] = top_cols[j, i] - change
         for j in range(k):
             part = product_nn(lower[OFF_AT[k, j]], inv[j * 4 + j])
             for m in range(j + 1, k):
@@ -439,21 +419,26 @@
             remote(sall.at[z - d], sall.at[z - d], zs.at[d], zr.at[d], sub, z).wait_recv()
             out_ref[...] += product_nt(sall[z - d], vz[z - d])
 
-    loop(1, 8, d1_copy, "wait_send")
-    loop(1, 4, d2_copy, "wait_send")
-    loop(1, 32, d3_copy, "wait_send")
-    scatter("wait_send")
-
-    @pl.when((holder < 6) & (y == 0))
-    def _():
-        loop(1, 4, fw_copy, "wait_send")
-
-    @pl.when(holder < 6)
-    def _():
-        loop(1, 32, oa_copy, "wait_send")
-
-    for r in range(4):
-        s0_copy(r).wait_send()
+    landed(gather1.at[0:7], d1s)
+    landed(gather2.at[0:3], d2s)
+    for ahead in range(4):
+        @pl.when(z + ahead < 4)
+        def _(ahead=ahead):
+            sent = top_cols.at[0, 0 : ahead + 1] if ahead else top_cols.at[0, 0, 0:112]
+            landed(sent, d3s.at[ahead])
+    for owner, column, low, high in SOURCES:
+        @pl.when((sub == owner) & (z == column))
+        def _(low=low, high=high):
+            landed(acc.at[0, 0, 0 : high - low, 0:112], sc_s)
+    for column in range(3):
+        @pl.when((z == column) & (y == 0))
+        def _(column=column):
+            for t in range(1, 4):
+                fw_copy(t, column).wait_send()
+
+    link_copy.wait_send()
+    for n in range(subs):
+        s0_copy(n).wait_send()
     for kind in range(6):
         for h in range(2):
             s1_copy(kind, h).wait_send()
@@ -470,7 +455,9 @@
     subs, cells, faces = coupling.shape[:3]
     blocks = lambda *lead: pltpu.VMEM((*lead, BLK, BLK), F32)
     dma = lambda n: pltpu.SemaphoreType.DMA((n,))
+    one = pltpu.SemaphoreType.DMA
     groups = subs * cells // GROUP
+    halves_of = interface.reshape(2, BLK, BLK)
     return pl.pallas_call(
         functools.partial(panel_kernel, 4),
         out_shape=jax.ShapeDtypeStruct(interface.shape, F32),
@@ -479,35 +466,33 @@
         scratch_shapes=[
             pltpu.SMEM(pattern.shape, jnp.int32),
             pltpu.SMEM(link.shape, jnp.int32),
-            pltpu.VMEM(interface.shape, F32),
+            pltpu.SMEM(link.shape, jnp.int32),
+            blocks(2),
             blocks(subs * cells),
             blocks(subs * cells, faces - 1),
             blocks(subs * cells),
             pltpu.VMEM((subs * cells, BLK, 2 * BLK), BF16),
             blocks(subs * (faces - 1) + 1),
+            blocks(subs * (faces - 1) + 1),
             dma(3), dma(groups), dma(groups), dma(groups),
             blocks(),
             pltpu.VMEM((8, 16, BLK), F32),
             pltpu.VMEM((4, 16, BLK), F32),
-            pltpu.VMEM((16, BLK), F32),
-            blocks(4),
-            pltpu.VMEM((32, BLK), F32),
-            blocks(6),
-            blocks(4, 2, 4), blocks(4, 2, 4), blocks(4, 2, 4),
-            blocks(2, 2), blocks(2, 2), blocks(2, 2), blocks(2, 2), blocks(2, 2), blocks(2, 2),
+            pltpu.VMEM((4, 16, BLK), F32),
+            blocks(4, 4),
+            blocks(4, 2, 4), blocks(2, 2), blocks(2, 2), blocks(2, 2), blocks(2, 2), blocks(2, 2), blocks(2, 2),
             blocks(6),
             pltpu.VMEM((4, 2 * BLK, BLK), F32),
             pltpu.VMEM((BLK, 2 * BLK), F32),
             blocks(6), blocks(16), blocks(4), blocks(),
-            dma(8), dma(8), dma(4), dma(4), dma(32), pltpu.SemaphoreType.DMA,
-            dma(24), pltpu.SemaphoreType.DMA, dma(4), dma(32), pltpu.SemaphoreType.DMA,
-            dma(4), dma(4), dma(12), dma(12), dma(6), dma(6), dma(4), dma(4),
+            one, one, one, one, dma(4), dma(4), one, one, dma(4),
+            dma(3), dma(3), dma(12), dma(12), dma(6), dma(6), dma(4), dma(4),
         ],
         compiler_params=pltpu.CompilerParams(
             collective_id=0, has_side_effects=True, vmem_limit_bytes=60 << 20
         ),
         name="panel_solve",
-    )(pattern, link, coupling, inverse, interface)
+    )(pattern, link, coupling, inverse, halves_of)
 
 
 def shards(coupling_blocks, block_inverse, coupling_pattern, link_blocks, interface_panel):

time: 54.3 us -> 47.5 us (0.87); the launches traced: 54.2 us -> 46.8 us
  Pallas kernels: 52.6 us -> 45.2 us
    pallas_call x1, Pallas kernels: 52.6 us -> 45.2 us  [panel_solve(): pl.pallas_call(functools.partial(panel_kernel, 4), out_shape=jax.ShapeDty...]
where the time goes in v3:
time: 47.5 us; the launch traced here: 46.8 us
  Pallas kernels  45.2 us (95%)
  local copies, waits for them, and re-layouts  1.57 us (3%)
    pallas_call x1, Pallas kernels, panel_solve(): pl.pallas_call(functools.partial(panel_kernel, 4), out_shape=jax.ShapeDty...  45.2 us
    unnamed x1, local copies, waits for them, and re-layouts  1.57 us

profile of v3, /device:TPU:64, one launch (start us, length us, event | category | flops | bytes accessed | tf_op | source)
XLA Modules:
  0.0 46.8 jit_solution(7546449501104321798)
XLA Ops:
  0.0 45.2 %panel_solve.1 = f32[256,128]{1,0:T(8,128)} custom-call(s32[9,2,16]{2,1,0:T(2,128)} %bitcast.3, s32[2,8]{1,0:T(2,128)} %link_ref.1, f32[2,16,9,128,128]{4,3,2,1,0:T(8,128)} %coupling_ref.1, f32[2,16,128,128]{3,2,1,0:T(8,128)} %inverse_ref.1, f32[2,128,128]{2,1,0:T(8,128)} %bitcast.2), custom_call_target="tpu_custom_call" | custom-call | tf_op jit(solution)/shard_map/panel_solve/pallas_call | solution.py:461
  45.2 1.6 %copy.7 = f32[256,128]{1,0:T(8,128)} copy(f32[256,128]{1,0:T(8,128)} %panel_solve.1) | data formatting | bytes 262144

commit v4 on v3

--- a/solution.py
+++ b/solution.py
@@ -13,8 +13,7 @@
 BLK = 128
 GROUP = 8
 STEP = 16
-OFF = ((1, 0), (2, 0), (3, 0), (2, 1), (3, 1), (3, 2))
-OFF_AT = {pair: k for k, pair in enumerate(OFF)}
+HALF = BLK // 2
 
 
 def halves(value):
@@ -48,14 +47,17 @@
     for r in range(0, BLK, STEP):
         pa, pe = pair[r : r + STEP, :BLK], pair[r : r + STEP, BLK:]
         t = jnp.stack([jnp.broadcast_to(pa[:, r + j : r + j + 1], (STEP, BLK)) for j in range(STEP)])
+        pivots = jnp.zeros((STEP, BLK), F32)
         for k in range(STEP):
-            scale = lax.rsqrt(t[0, k : k + 1, :])
-            m = jnp.where(rows > k, t[0] * scale, 0.0)
+            pivot = t[0, k : k + 1, :]
+            m = jnp.where(rows > k, t[0] * (1.0 / pivot), 0.0)
+            pivots = jnp.where(rows == k, pivot, pivots)
             if k + 1 < STEP:
-                t = t[1:] - m[None] * (t[1:, k : k + 1, :] * scale[None])
-            ra, re = pa[k : k + 1] * scale, pe[k : k + 1] * scale
-            pa = jnp.where(rows == k, ra, pa - m * ra)
-            pe = jnp.where(rows == k, re, pe - m * re)
+                t = t[1:] - m[None] * t[1:, k : k + 1, :]
+            pa = pa - m * pa[k : k + 1]
+            pe = pe - m * pe[k : k + 1]
+        scale = lax.rsqrt(pivots)
+        pa, pe = pa * scale, pe * scale
         pair[r : r + STEP, BLK:] = pe
         if r + STEP < BLK:
             high, low = halves(jnp.concatenate([pa, pe], axis=1))
@@ -75,10 +77,9 @@
     pattern, link, peer_link, panel_ref, firsts, faces, inverses, rhs, links_ref, peer_links,
     small_s, inv_s, first_s, face_s,
     firstc, gather1, gather2, pieces, top_cols,
-    acc, relay_r, relay_l, direct_r, direct_l, onward_r, onward_l,
-    last, sall, pair, lower, inv, vz, top,
-    d1s, d1r, d2s, d2r, d3s, d3r, sc_s, op_r, fw_s,
-    s0s, s0r, s1s, s1r, s2s, s2r, zs, zr,
+    acc, inflow, last, sall, pair, lower, inv, above, own_above, own_w, rest, top,
+    d1s, d1r, d2s, d2r, d3s, d3r, of_s, of_r, sw_s, sw_r, sc_s, op_r, fw_s,
+    s0s, s0r, s1s, s1a, s1b, s2s, s2r, zs, zr,
 ):
     sub, z = lax.axis_index("sub"), lax.axis_index("blk")
     core = lax.rem(sub, 2)
@@ -251,31 +252,59 @@
 
     landed(gather2.at[0:3], d2r)
     pieces[z] = jnp.sum(gather2[...], axis=0)
-    for column in range(3):
-        @pl.when((z == column) & (y > 0))
-        def _(column=column):
-            landed(pieces.at[column + 1 : 4], op_r)
-
     pltpu.make_async_copy(pieces.at[z], top_cols.at[z, z, mine], d3r.at[z]).start()
     for ahead in range(3, -1, -1):
         @pl.when(z + ahead < 4)
         def _(ahead=ahead):
-            part = pl.ds(z, ahead + 1)
-
             def send(t, carry):
                 remote(
-                    pieces.at[part], top_cols.at[z, part, mine], d3s.at[ahead], d3r.at[z],
+                    pieces.at[z], top_cols.at[z, z, mine], d3s.at[ahead], d3r.at[z],
                     row_peer(t)[1], z + ahead,
                 ).start()
                 return carry
 
             lax.fori_loop(0 if ahead else 1, 8, send, 0)
 
-    def column_arrives(j):
-        for row in range(j, 4):
+    def below_send():
+        for column in range(3):
+            @pl.when((z == column) & (y > 0))
+            def _(column=column):
+                landed(pieces.at[column + 1 : 4], op_r)
+
+        for ahead in range(3, 0, -1):
+            @pl.when(z + ahead < 4)
+            def _(ahead=ahead):
+                part = pl.ds(z + 1, ahead)
+                for xx in range(4):
+                    remote(
+                        pieces.at[part], top_cols.at[z, part, mine], of_s.at[ahead], of_r.at[z],
+                        sub_of(y, xx, core), z + ahead,
+                    ).start()
+
+    own_half = pl.ds(pl.multiple_of(core * HALF, HALF), HALF)
+
+    def swap_copy(j, row):
+        part = top_cols.at[j, j + 1 : row + 1, own_half]
+        return remote(part, part, sw_s.at[j], sw_r.at[j], peer, z)
+
+    def each_below(act):
+        for row in range(1, 4):
             @pl.when(z == row)
             def _(row=row):
-                landed(top_cols.at[j, j : row + 1], d3r.at[j])
+                for j in range(row):
+                    act(j, row)
+
+    def below_swap():
+        def act(j, row):
+            landed(top_cols.at[j, j + 1 : row + 1, 0:HALF], of_r.at[j])
+            swap_copy(j, row).start()
+
+        each_below(act)
+
+    def diagonal_arrives(j):
+        @pl.when(z >= j)
+        def _():
+            landed(top_cols.at[j, j], d3r.at[j])
 
     link_copy.wait_recv()
     names = [[link[n, l] for l in range(links)] for n in range(subs)]
@@ -308,124 +337,155 @@
             return sub_of(y, lax.rem(x + step + 4, 4), core)
         return sub_of(lax.rem(y + step + 4, 4), x, core)
 
-    def s1_copy(kind, h):
-        n = kind * 2 + h
-        src, dst, step = (
-            (acc.at[2, h, 0:2], relay_r.at[h], 1),
-            (acc.at[2, h, 2:4], relay_l.at[h], -1),
-            (acc.at[1, h, 2:4], direct_r.at[h], 1),
-            (acc.at[3, h, 0:2], direct_l.at[h], -1),
-            (acc.at[1, h, 0:2], onward_r.at[h], 1),
-            (acc.at[3, h, 2:4], onward_l.at[h], -1),
-        )[kind]
-        return remote(src, dst, s1s.at[n], s1r.at[n], ring(h, step), z)
+    def rows_of(c):
+        return pl.ds(c * HALF, HALF)
+
+    def s1_start(kinds, c):
+        rows = rows_of(c)
+        for kind in kinds:
+            r, low, step = ((2, 0, 1), (2, 2, -1), (1, 2, 1), (3, 0, -1), (1, 0, 1), (3, 2, -1))[kind]
+            for h in range(2):
+                remote(
+                    acc.at[r, h, low : low + 2, rows], inflow.at[kind, h, 0:2, rows],
+                    s1s, (s1a if kind < 2 else s1b).at[c], ring(h, step), z,
+                ).start()
 
     for n in range(subs):
         s0_copy(n).wait_recv()
-    for r, kinds in ((2, (0, 1)), (1, (2,)), (3, (3,)), (0, ())):
-        fill(r)
-        for kind in kinds:
-            for h in range(2):
-                s1_copy(kind, h).start()
-
-    def service1():
+    fill(2)
+    s1_start((0, 1), 0)
+    fill(1)
+    fill(3)
+    s1_start((2, 3), 0)
+    s1_start((0, 1), 1)
+    s1_start((2, 3), 1)
+    below_send()
+    fill(0)
+
+    def service1(c):
+        rows = rows_of(c)
+        landed(inflow.at[0:2, 0:2, 0:2, rows], s1a.at[c])
         for h in range(2):
-            s1_copy(0, h).wait_recv()
-            acc[1, h, 0:2] += relay_r[h]
-            s1_copy(4, h).start()
-            s1_copy(1, h).wait_recv()
-            acc[3, h, 2:4] += relay_l[h]
-            s1_copy(5, h).start()
-
-    def s2_copy(h, d):
-        there = lax.rem((y if h == 0 else x) + d, 4)
-        to = sub_of(there, x, core) if h == 0 else sub_of(y, there, core)
-        n = h * 3 + d - 1
-        return remote(acc.at[0, h, there], last.at[n], s2s.at[n], s2r.at[n], to, z)
-
-    def service2():
+            acc[1, h, 0:2, rows] += inflow[0, h, 0:2, rows]
+            acc[3, h, 2:4, rows] += inflow[1, h, 0:2, rows]
+        s1_start((4, 5), c)
+
+    def service2(c):
+        rows = rows_of(c)
+        landed(inflow.at[2:6, 0:2, 0:2, rows], s1b.at[c])
         for h in range(2):
-            s1_copy(4, h).wait_recv()
-            s1_copy(3, h).wait_recv()
-            acc[0, h, 0:2] += onward_r[h] + direct_l[h]
-            s1_copy(2, h).wait_recv()
-            s1_copy(5, h).wait_recv()
-            acc[0, h, 2:4] += direct_r[h] + onward_l[h]
+            acc[0, h, 0:2, rows] += inflow[3, h, 0:2, rows] + inflow[4, h, 0:2, rows]
+            acc[0, h, 2:4, rows] += inflow[2, h, 0:2, rows] + inflow[5, h, 0:2, rows]
             for d in range(1, 4):
-                s2_copy(h, d).start()
-
-    def z_copy(d):
-        return remote(sall.at[z], sall.at[z], zs.at[d], zr.at[d], sub, z + d)
-
-    def service3():
+                there = lax.rem((y if h == 0 else x) + d, 4)
+                to = sub_of(there, x, core) if h == 0 else sub_of(y, there, core)
+                remote(
+                    acc.at[0, h, there, rows], last.at[h * 3 + d - 1, rows], s2s, s2r.at[c], to, z
+                ).start()
+
+    def z_copy(d, c, base):
+        part = sall.at[base, 0:2, rows_of(c)]
+        return remote(part, part, zs, zr.at[d], sub, base + d)
+
+    def service3(c):
+        rows = rows_of(c)
+        landed(last.at[0:6, rows], s2r.at[c])
         for h in range(2):
-            total = acc[0, h, y if h == 0 else x]
+            total = acc[0, h, y if h == 0 else x, rows]
             for d in range(1, 4):
-                s2_copy(h, d).wait_recv()
-                total = total + last[h * 3 + d - 1]
-            rows = panel_ref[h] - total
-            sall[z, h * BLK : (h + 1) * BLK] = rows
-
-            @pl.when(sub * 2 + h == z)
-            def _():
-                sall[z, h * BLK : (h + 1) * BLK] = top[...]
-
-        for d in range(1, 4):
+                total = total + last[h * 3 + d - 1, rows]
+            sall[z, h, rows] = jnp.where(sub * 2 + h == z, top[rows], panel_ref[h, rows] - total)
+
+        for d in range(3, 0, -1):
             @pl.when(z + d < 4)
             def _():
-                z_copy(d).start()
-
-    column_arrives(0)
+                z_copy(d, c, z).start()
+
+    def earlier_columns():
+        rest[...] = sall[z].reshape(2 * BLK, BLK)
+        for d in range(1, 4):
+            @pl.when(z >= d)
+            def _():
+                landed(sall.at[z - d], zr.at[d])
+                column = pl.ds(pl.multiple_of((z - d) * BLK, BLK), BLK)
+                rest[...] -= product_nt(sall[z - d].reshape(2 * BLK, BLK), own_above[:, column])
+
+    diagonal_arrives(0)
     unit = jnp.where(
         lax.broadcasted_iota(jnp.int32, (BLK, BLK), 0) == lax.broadcasted_iota(jnp.int32, (BLK, BLK), 1),
         1.0, 0.0,
     )
+    inv[...] = jnp.zeros_like(inv)
     hooks = {
-        (0, 3): service1,
-        (1, 3): service2,
-        (2, 4): service3,
+        (0, 3): lambda: service1(0),
+        (0, 6): below_swap,
+        (0, 7): lambda: service1(1),
+        (1, 3): lambda: service2(0),
+        (1, 7): lambda: service2(1),
+        (2, 4): lambda: service3(0),
+        (3, 0): lambda: service3(1),
+        (3, 7): earlier_columns,
     }
+
+    def row_of_inverse(k):
+        if k:
+            width = slice(0, k * BLK)
+            inv[k * BLK : (k + 1) * BLK, width] = -product_nn(
+                inv[k * BLK : (k + 1) * BLK, k * BLK : (k + 1) * BLK], above[:, width]
+            )
+
+    def subtract(k, j):
+        left = lower[j:4, :, k * BLK : (k + 1) * BLK].reshape((4 - j) * BLK, BLK)
+        change = product_nt(left, lower[j, :, k * BLK : (k + 1) * BLK])
+        top_cols[j, j:4] = top_cols[j, j:4] - change.reshape(4 - j, BLK, BLK)
+
+    def between(k, r):
+        if k and r == 0:
+            for j in range(k + 1, 4):
+                subtract(k - 1, j)
+            row_of_inverse(k - 1)
+        if k and r == 2:
+            width = slice(0, k * BLK)
+            above[:, width] = product_nn(lower[k, :, width], inv[width, width])
+
+            @pl.when(z == k)
+            def _():
+                own_above[...] = above[...]
+        if (k, r) in hooks:
+            hooks[k, r]()
+
     for k in range(4):
         pair[:, :BLK] = top_cols[k, k]
         pair[:, BLK:] = unit
-        inverse_factor(pair, lambda r, k=k: hooks.get((k, r), lambda: None)())
+        inverse_factor(pair, functools.partial(between, k))
         w = pair[:, BLK:]
+
+        @pl.when(z == k)
+        def _():
+            own_w[...] = w
+
+        inv[k * BLK : (k + 1) * BLK, k * BLK : (k + 1) * BLK] = w
         if k == 0:
             for j in range(1, 4):
-                column_arrives(j)
+                diagonal_arrives(j)
+            each_below(lambda j, row: swap_copy(j, row).wait())
             top[...] = top_cols[z, z]
-        for i in range(k + 1, 4):
-            lower[OFF_AT[i, k]] = product_nt(top_cols[k, i], w)
-        for i in range(k + 1, 4):
-            for j in range(k + 1, i + 1):
-                change = product_nt(lower[OFF_AT[i, k]], lower[OFF_AT[j, k]])
-                top_cols[j, i] = top_cols[j, i] - change
-        for j in range(k):
-            part = product_nn(lower[OFF_AT[k, j]], inv[j * 4 + j])
-            for m in range(j + 1, k):
-                part = part + product_nn(lower[OFF_AT[k, m]], inv[m * 4 + j])
-            inv[k * 4 + j] = -product_nn(w, part)
-        inv[k * 4 + k] = w
-
-        @pl.when(z == k)
-        def _():
-            for j in range(k + 1):
-                vz[j] = inv[k * 4 + j]
-
-    out_ref[...] = product_nt(sall[z], vz[z])
-    for d in range(1, 4):
-        @pl.when(z >= d)
-        def _():
-            remote(sall.at[z - d], sall.at[z - d], zs.at[d], zr.at[d], sub, z).wait_recv()
-            out_ref[...] += product_nt(sall[z - d], vz[z - d])
+        if k < 3:
+            stack = top_cols[k, k + 1 : 4].reshape((3 - k) * BLK, BLK)
+            lower[k + 1 : 4, :, k * BLK : (k + 1) * BLK] = product_nt(stack, w).reshape(3 - k, BLK, BLK)
+            subtract(k, k + 1)
+
+    out_ref[...] = product_nt(rest[...], own_w[...]).reshape(2, BLK, BLK)
 
     landed(gather1.at[0:7], d1s)
     landed(gather2.at[0:3], d2s)
     for ahead in range(4):
         @pl.when(z + ahead < 4)
         def _(ahead=ahead):
-            sent = top_cols.at[0, 0 : ahead + 1] if ahead else top_cols.at[0, 0, 0:112]
+            sent = top_cols.at[0, 0] if ahead else top_cols.at[0, 0, 0:112]
             landed(sent, d3s.at[ahead])
+            if ahead:
+                landed(top_cols.at[0, 0:ahead, 0:HALF], of_s.at[ahead])
     for owner, column, low, high in SOURCES:
         @pl.when((sub == owner) & (z == column))
         def _(low=low, high=high):
@@ -439,16 +499,12 @@
     link_copy.wait_send()
     for n in range(subs):
         s0_copy(n).wait_send()
-    for kind in range(6):
-        for h in range(2):
-            s1_copy(kind, h).wait_send()
-    for h in range(2):
-        for d in range(1, 4):
-            s2_copy(h, d).wait_send()
-    for d in range(1, 4):
-        @pl.when(z + d < 4)
-        def _():
-            z_copy(d).wait_send()
+    landed(inflow, s1s)
+    landed(last, s2s)
+    for row in range(3):
+        @pl.when(z == row)
+        def _(row=row):
+            landed(sall.at[0 : 3 - row], zs)
 
 
 def panel_solve(pattern, link, coupling, inverse, interface):
@@ -460,7 +516,7 @@
     halves_of = interface.reshape(2, BLK, BLK)
     return pl.pallas_call(
         functools.partial(panel_kernel, 4),
-        out_shape=jax.ShapeDtypeStruct(interface.shape, F32),
+        out_shape=jax.ShapeDtypeStruct((2, BLK, BLK), F32),
         in_specs=[pl.BlockSpec(memory_space=pltpu.HBM)] * 5,
         out_specs=pl.BlockSpec(memory_space=pltpu.VMEM),
         scratch_shapes=[
@@ -480,19 +536,25 @@
             pltpu.VMEM((4, 16, BLK), F32),
             pltpu.VMEM((4, 16, BLK), F32),
             blocks(4, 4),
-            blocks(4, 2, 4), blocks(2, 2), blocks(2, 2), blocks(2, 2), blocks(2, 2), blocks(2, 2), blocks(2, 2),
+            blocks(4, 2, 4), blocks(6, 2, 2),
             blocks(6),
-            pltpu.VMEM((4, 2 * BLK, BLK), F32),
+            blocks(4, 2),
             pltpu.VMEM((BLK, 2 * BLK), F32),
-            blocks(6), blocks(16), blocks(4), blocks(),
-            one, one, one, one, dma(4), dma(4), one, one, dma(4),
-            dma(3), dma(3), dma(12), dma(12), dma(6), dma(6), dma(4), dma(4),
+            pltpu.VMEM((4, BLK, 4 * BLK), F32),
+            pltpu.VMEM((4 * BLK, 4 * BLK), F32),
+            pltpu.VMEM((BLK, 4 * BLK), F32),
+            pltpu.VMEM((BLK, 4 * BLK), F32),
+            blocks(),
+            pltpu.VMEM((2 * BLK, BLK), F32),
+            blocks(),
+            one, one, one, one, dma(4), dma(4), dma(4), dma(4), dma(4), dma(4), one, one, dma(4),
+            dma(3), dma(3), one, dma(2), dma(2), one, dma(2), one, dma(4),
         ],
         compiler_params=pltpu.CompilerParams(
             collective_id=0, has_side_effects=True, vmem_limit_bytes=60 << 20
         ),
         name="panel_solve",
-    )(pattern, link, coupling, inverse, halves_of)
+    )(pattern, link, coupling, inverse, halves_of).reshape(interface.shape)
 
 
 def shards(coupling_blocks, block_inverse, coupling_pattern, link_blocks, interface_panel):

time: 47.5 us -> 45.4 us (0.956)
  Pallas kernels: 45.2 us -> 43.4 us
    pallas_call x1, Pallas kernels: 45.2 us -> 43.4 us  [panel_solve(): pl.pallas_call(functools.partial(panel_kernel, 4), out_shape=jax.ShapeDty...]
where the time goes in v4:
time: 45.4 us; the launch traced here: 44.9 us
  Pallas kernels  43.4 us (96%)
  local copies, waits for them, and re-layouts  1.57 us (3%)
    pallas_call x1, Pallas kernels, panel_solve(): pl.pallas_call(functools.partial(panel_kernel, 4), out_shape=jax.ShapeDty...  43.4 us
    unnamed x1, local copies, waits for them, and re-layouts  1.57 us

profile of v4, /device:TPU:64, one launch (start us, length us, event | category | flops | bytes accessed | tf_op | source)
XLA Modules:
  0.0 44.9 jit_solution(9648238207060390248)
XLA Ops:
  0.0 43.4 %panel_solve.1 = f32[2,128,128]{2,1,0:T(8,128)} custom-call(s32[9,2,16]{2,1,0:T(2,128)} %bitcast.5, s32[2,8]{1,0:T(2,128)} %link_ref.1, f32[2,16,9,128,128]{4,3,2,1,0:T(8,128)} %coupling_ref.1, f32[2,16,128,128]{3,2,1,0:T(8,128)} %inverse_ref.1, f32[2,128,128]{2,1,0:T(8,128)} %bitcast.4), custom_call_target="tpu_custom_call" | custom-call | tf_op jit(solution)/shard_map/panel_solve/pallas_call | solution.py:517
  43.4 1.6 %copy.7 = f32[256,128]{1,0:T(8,128)} copy(f32[256,128]{1,0:T(8,128)} %bitcast.3) | data formatting | bytes 262144
